TPU v7x, 128 devices: a whole 4x4x4 slice. The times are simulated.
128 devices in a mesh: dp: 32 (over x, y, core), seq: 4 (over z).
Axes of the slice: x: 4, y: 4, z: 4, core: 2. Of those that a mesh axis runs over, the one named last changes fastest.
Arguments:
- tokens: bfloat16 [32768, 1024], P(('dp', 'seq')), may hold values from -6 to 6
- routes: int32 [32768, 8], P(('dp', 'seq')), may hold values from 0 to 31, all different within a row; in each aligned block of 256 rows (0 to 255, 256 to 511, ...) at most 96 rows name the same one
- lengths: int32 [32], P('dp'), may hold values from 769 to 1024, as said below
- out_grad: bfloat16 [32768, 1024], P(('dp', 'seq')), may hold values from -6 to 6
- query_weight: float32 [1024, 1024], P(('dp', 'seq')), may hold values from -0.1875 to 0.1875
- query_mean: float32 [1024, 1024], P(('dp', 'seq')), may hold values from -128 to 128
- query_square: float32 [1024, 1024], P(('dp', 'seq')), may hold values from 1736.704 to 6881.28
- keyval_weight: float32 [1024, 1024], P(('dp', 'seq')), may hold values from -0.1875 to 0.1875
- keyval_mean: float32 [1024, 1024], P(('dp', 'seq')), may hold values from -128 to 128
- keyval_square: float32 [1024, 1024], P(('dp', 'seq')), may hold values from 1736.704 to 6881.28
- output_weight: float32 [1024, 1024], P(('dp', 'seq')), may hold values from -4 to 4
- output_mean: float32 [1024, 1024], P(('dp', 'seq')), may hold values from -4 to 4
- output_square: float32 [1024, 1024], P(('dp', 'seq')), may hold values from 3.2 to 12.8
- router_weight: float32 [1024, 32], P(('dp', 'seq')), may hold values from -0.09375 to 0.09375
- router_mean: float32 [1024, 32], P(('dp', 'seq')), may hold values from -256 to 256
- router_square: float32 [1024, 32], P(('dp', 'seq')), may hold values from 6881.28 to 27525.12
- norm_gains: float32 [2, 1024], P(None, ('dp', 'seq')), may hold values from 0.5 to 1.5
- gains_mean: float32 [2, 1024], P(None, ('dp', 'seq')), may hold values from -256 to 256
- gains_square: float32 [2, 1024], P(None, ('dp', 'seq')), may hold values from 6881.28 to 27525.12
- gateup_weight: float32 [32, 1024, 1024], P('dp', 'seq'), may hold values from -0.1875 to 0.1875
- gateup_mean: float32 [32, 1024, 1024], P('dp', 'seq'), may hold values from -14 to 14
- gateup_square: float32 [32, 1024, 1024], P('dp', 'seq'), may hold values from 24.90368 to 98.304
- down_weight: float32 [32, 512, 1024], P('dp', 'seq'), may hold values from -0.75 to 0.75
- down_mean: float32 [32, 512, 1024], P('dp', 'seq'), may hold values from -4 to 4
- down_square: float32 [32, 512, 1024], P('dp', 'seq'), may hold values from 1.540096 to 6.22592
Outputs:
- layer_out: bfloat16 [32768, 1024], P(('dp', 'seq'))
- tokens_grad: float32 [32768, 1024], P(('dp', 'seq'))
- query_updated: float32 [1024, 1024], P(('dp', 'seq'))
- querymean_new: float32 [1024, 1024], P(('dp', 'seq'))
- querysquare_new: float32 [1024, 1024], P(('dp', 'seq'))
- keyval_updated: float32 [1024, 1024], P(('dp', 'seq'))
- keyvalmean_new: float32 [1024, 1024], P(('dp', 'seq'))
- keyvalsquare_new: float32 [1024, 1024], P(('dp', 'seq'))
- output_updated: float32 [1024, 1024], P(('dp', 'seq'))
- outputmean_new: float32 [1024, 1024], P(('dp', 'seq'))
- outputsquare_new: float32 [1024, 1024], P(('dp', 'seq'))
- router_updated: float32 [1024, 32], P(('dp', 'seq'))
- routermean_new: float32 [1024, 32], P(('dp', 'seq'))
- routersquare_new: float32 [1024, 32], P(('dp', 'seq'))
- gains_updated: float32 [2, 1024], P(None, ('dp', 'seq'))
- gainsmean_new: float32 [2, 1024], P(None, ('dp', 'seq'))
- gainssquare_new: float32 [2, 1024], P(None, ('dp', 'seq'))
- gateup_updated: float32 [32, 1024, 1024], P('dp', 'seq')
- gateupmean_new: float32 [32, 1024, 1024], P('dp', 'seq')
- gateupsquare_new: float32 [32, 1024, 1024], P('dp', 'seq')
- down_updated: float32 [32, 512, 1024], P('dp', 'seq')
- downmean_new: float32 [32, 512, 1024], P('dp', 'seq')
- downsquare_new: float32 [32, 512, 1024], P('dp', 'seq')
Inputs may be any that keep to these rules, and one draw needn't show every extreme that they name: `routes`: in the rows of one device no expert is named by more than 96 rows. `lengths`: one sequence has length 1024.
All inputs are finite; a program needn't handle non-finite values.
Results may differ from a plain program's by a relative error of at most 0.029.
Values may be sent and summed in bfloat16 or wider, within the bound.
A program may use at most 256 MiB of HBM per device.

v0:
```python
import jax
import jax.numpy as jnp
from jax import lax
from jax.sharding import PartitionSpec as P

D = 1024
HEADS = 16
KV_HEADS = 8
HEAD_DIM = 64
EXPERTS = 32
TOP = 8
FF_E = 512
STEP = 10
CAP = 96


norm_epsilon = 1e-06
beta_first = 0.9
beta_second = 0.95
adam_epsilon = 1e-08
masked_score = -1e30


def rotary_tables(positions, half_width):
    freqs = 10000.0 ** (-jnp.arange(half_width, dtype=jnp.float32) / half_width)
    angles = positions.astype(jnp.float32)[:, None] * freqs[None, :]
    cosines = jnp.cos(angles)
    sines = jnp.sin(angles)
    return (jnp.concatenate([cosines, cosines], 1), jnp.concatenate([sines, sines], 1))


def rotate(values, cosines, sines):
    half_width = values.shape[-1] // 2
    turned = jnp.concatenate([-values[..., half_width:], values[..., :half_width]], -1)
    return values * cosines[:, None, :] + turned * sines[:, None, :]


def rotate_back(grads, cosines, sines):
    half_width = grads.shape[-1] // 2
    scaled = grads * sines[:, None, :]
    return grads * cosines[:, None, :] + jnp.concatenate(
        [scaled[..., half_width:], -scaled[..., :half_width]], -1
    )


def rms_scale(values):
    return lax.rsqrt(jnp.mean(values * values, axis=-1, keepdims=True) + norm_epsilon)


def norm_back(values, scale, gain, dnormed):
    scaled = values * scale
    dgain = jnp.sum(dnormed * scaled, axis=0)
    dscaled = dnormed * gain
    dvalues = scale * (dscaled - scaled * jnp.mean(dscaled * scaled, axis=-1, keepdims=True))
    return (dvalues, dgain)


def masked_scores(grouped, whole_kv, positions, length):
    key_count = whole_kv.shape[0]
    key_width = whole_kv.shape[1] // 2
    heads_kv = grouped.shape[1]
    head_size = grouped.shape[3]
    all_keys = whole_kv[:, :key_width].reshape(key_count, heads_kv, head_size)
    all_values = whole_kv[:, key_width:].reshape(key_count, heads_kv, head_size)
    raw_scores = jnp.einsum(
        "qkgd,pkd->kgqp", grouped, all_keys, preferred_element_type=jnp.float32
    ) * head_size ** (-0.5)
    key_pos = jnp.arange(key_count, dtype=jnp.int32)
    allowed = (key_pos[None, :] <= positions[:, None]) & (key_pos[None, :] < length)
    return (jnp.where(allowed, raw_scores, masked_score), all_keys, all_values)


def adamw(weight, grad, first, second, rate, decay):
    first_new = beta_first * first + (1.0 - beta_first) * grad
    second_new = beta_second * second + (1.0 - beta_second) * grad * grad
    update = (
        first_new
        / (1.0 - beta_first**STEP)
        / (jnp.sqrt(second_new / (1.0 - beta_second**STEP)) + adam_epsilon)
    )
    return (weight - rate * (update + decay * weight), first_new, second_new)


def body(
    tokens,
    routes,
    lengths,
    out_grad,
    query_weight,
    query_mean,
    query_square,
    keyval_weight,
    keyval_mean,
    keyval_square,
    output_weight,
    output_mean,
    output_square,
    router_weight,
    router_mean,
    router_square,
    norm_gains,
    gains_mean,
    gains_square,
    gateup_weight,
    gateup_mean,
    gateup_square,
    down_weight,
    down_mean,
    down_square,
):
    bfloat = jnp.bfloat16
    single = jnp.float32
    row_count = tokens.shape[0]
    seq_len = row_count * lax.axis_size("seq")
    positions = lax.axis_index("seq") * row_count + jnp.arange(row_count, dtype=jnp.int32)
    length = lengths[0]
    key_width = KV_HEADS * HEAD_DIM
    query_width = HEADS * HEAD_DIM
    group_size = HEADS // KV_HEADS
    head_scale = HEAD_DIM ** (-0.5)
    query_b, keyval_b, output_b, router_b, gains_b = (
        lax.all_gather(query_weight.astype(bfloat), ("dp", "seq"), axis=0, tiled=True),
        lax.all_gather(keyval_weight.astype(bfloat), ("dp", "seq"), axis=0, tiled=True),
        lax.all_gather(output_weight.astype(bfloat), ("dp", "seq"), axis=0, tiled=True),
        lax.all_gather(router_weight.astype(bfloat), ("dp", "seq"), axis=0, tiled=True),
        lax.all_gather(norm_gains.astype(bfloat), ("dp", "seq"), axis=1, tiled=True),
    )
    gateup_b, down_b = (
        lax.all_gather(gateup_weight.astype(bfloat), "seq", axis=1, tiled=True),
        lax.all_gather(down_weight.astype(bfloat), "seq", axis=1, tiled=True),
    )
    gains_f = gains_b.astype(single)
    inputs = tokens.astype(single)
    scale_one = rms_scale(inputs)
    normed = (inputs * scale_one * gains_f[0]).astype(bfloat)
    queries = jnp.dot(normed, query_b, preferred_element_type=single)
    keyvals = jnp.dot(normed, keyval_b, preferred_element_type=single)
    cosines, sines = rotary_tables(positions, HEAD_DIM // 2)
    rotated_q = rotate(queries.reshape(row_count, HEADS, HEAD_DIM), cosines, sines).astype(bfloat)
    rotated_k = rotate(
        keyvals[:, :key_width].reshape(row_count, KV_HEADS, HEAD_DIM), cosines, sines
    ).astype(bfloat)
    local_kv = jnp.concatenate(
        [rotated_k.reshape(row_count, key_width), keyvals[:, key_width:].astype(bfloat)], 1
    )
    whole_kv = lax.all_gather(local_kv, "seq", axis=0, tiled=True)
    grouped = rotated_q.reshape(row_count, KV_HEADS, group_size, HEAD_DIM)
    scores, all_keys, all_values = masked_scores(grouped, whole_kv, positions, length)
    top_score = jnp.max(scores, axis=-1, keepdims=True)
    log_total = top_score + jnp.log(jnp.sum(jnp.exp(scores - top_score), axis=-1, keepdims=True))
    attention = jnp.exp(scores - log_total)
    mixed_heads = jnp.einsum(
        "kgqp,pkd->qkgd", attention.astype(bfloat), all_values, preferred_element_type=single
    )
    heads_out = mixed_heads.reshape(row_count, query_width).astype(bfloat)
    residual = inputs + jnp.dot(heads_out, output_b, preferred_element_type=single)
    scale_two = rms_scale(residual)
    normed_two = (residual * scale_two * gains_f[1]).astype(bfloat)
    logits = jnp.dot(normed_two, router_b, preferred_element_type=single)
    expert_ids = jnp.arange(EXPERTS, dtype=jnp.int32)
    route_hits = routes[:, :, None] == expert_ids[None, None, :]
    chosen = jnp.sum(jnp.where(route_hits, logits[:, None, :], 0.0), axis=2)
    gate_probs = jax.nn.softmax(chosen, axis=-1)
    flat_hits = route_hits.reshape(-1, EXPERTS).astype(jnp.int32)
    slot_ranks = jnp.sum((jnp.cumsum(flat_hits, axis=0) - 1) * flat_hits, axis=1)
    slot_index = routes.reshape(-1) * CAP + slot_ranks
    pair_count = slot_index.shape[0]
    source = (
        jnp.full((EXPERTS * CAP,), -1, jnp.int32)
        .at[slot_index]
        .set(jnp.arange(pair_count, dtype=jnp.int32))
    )
    filled = source >= 0
    source_pair = jnp.maximum(source, 0)
    source_token = source_pair // TOP
    model_width = normed_two.shape[1]
    send_rows = jnp.where(filled[:, None], normed_two[source_token], jnp.zeros((), bfloat)).reshape(
        EXPERTS, CAP, model_width
    )
    out_single = out_grad.astype(single)
    gate_flat = gate_probs.reshape(-1)
    slot_grads = jnp.where(
        filled[:, None], gate_flat[source_pair][:, None] * out_single[source_token], 0.0
    )
    slot_grads = slot_grads.astype(bfloat).reshape(EXPERTS, CAP, model_width)
    received = lax.all_to_all(send_rows, "dp", split_axis=0, concat_axis=1, tiled=True)
    gateup = jnp.einsum("erd,edf->erf", received, gateup_b, preferred_element_type=single)
    hidden = (jax.nn.silu(gateup[..., :FF_E]) * gateup[..., FF_E:]).astype(bfloat)
    expert_out = jnp.einsum("erf,efd->erd", hidden, down_b, preferred_element_type=single).astype(
        bfloat
    )
    returned = lax.all_to_all(expert_out, "dp", split_axis=1, concat_axis=0, tiled=True)
    picked = returned.reshape(EXPERTS * CAP, model_width)[slot_index].reshape(
        row_count, TOP, model_width
    )
    layer_sum = residual + jnp.sum(gate_probs[:, :, None] * picked.astype(single), axis=1)
    layer_out = layer_sum.astype(bfloat)
    dgates = jnp.einsum("rkd,rd->rk", picked, out_grad, preferred_element_type=single)
    dchosen = gate_probs * (dgates - jnp.sum(gate_probs * dgates, axis=-1, keepdims=True))
    dlogits = jnp.sum(jnp.where(route_hits, dchosen[:, :, None], 0.0), axis=1).astype(bfloat)
    expert_grads_in = lax.all_to_all(slot_grads, "dp", split_axis=0, concat_axis=1, tiled=True)
    gateup_again = jnp.einsum("erd,edf->erf", received, gateup_b, preferred_element_type=single)
    gate_part = gateup_again[..., :FF_E]
    up_part = gateup_again[..., FF_E:]
    hidden_again = (jax.nn.silu(gate_part) * up_part).astype(bfloat)
    sigmoid_gate = jax.nn.sigmoid(gate_part)
    activated = gate_part * sigmoid_gate
    d_down = jnp.einsum(
        "erf,erd->efd", hidden_again, expert_grads_in, preferred_element_type=single
    )
    dhidden = jnp.einsum("erd,efd->erf", expert_grads_in, down_b, preferred_element_type=single)
    dgate_part = dhidden * up_part * (sigmoid_gate * (1.0 + gate_part * (1.0 - sigmoid_gate)))
    dup_part = dhidden * activated
    dgateup = jnp.concatenate([dgate_part, dup_part], -1).astype(bfloat)
    d_gateup = jnp.einsum("erd,erf->edf", received, dgateup, preferred_element_type=single)
    drows = jnp.einsum("erf,edf->erd", dgateup, gateup_b, preferred_element_type=single).astype(
        bfloat
    )
    back_rows = lax.all_to_all(drows, "dp", split_axis=1, concat_axis=0, tiled=True)
    gathered_back = back_rows.reshape(EXPERTS * CAP, model_width)[slot_index].reshape(
        row_count, TOP, model_width
    )
    dnormed_two = jnp.sum(gathered_back.astype(single), axis=1) + jnp.dot(
        dlogits, router_b.T, preferred_element_type=single
    )
    d_router = jnp.dot(normed_two.T, dlogits, preferred_element_type=single)
    dnorm_two, dgain_two = norm_back(residual, scale_two, gains_f[1], dnormed_two)
    dresidual = out_single + dnorm_two
    dattended = dresidual.astype(bfloat)
    d_output = jnp.dot(heads_out.T, dattended, preferred_element_type=single)
    dmixed = jnp.dot(dattended, output_b.T, preferred_element_type=single).astype(bfloat)
    scores_back, keys_back, values_back = masked_scores(grouped, whole_kv, positions, length)
    attention_back = jnp.exp(scores_back - log_total)
    dmixed_grouped = dmixed.reshape(row_count, KV_HEADS, group_size, HEAD_DIM)
    dattention = jnp.einsum(
        "qkgd,pkd->kgqp", dmixed_grouped, values_back, preferred_element_type=single
    )
    d_values = jnp.einsum(
        "kgqp,qkgd->pkd",
        attention_back.astype(bfloat),
        dmixed_grouped,
        preferred_element_type=single,
    )
    dscores = attention_back * (
        dattention - jnp.sum(attention_back * dattention, axis=-1, keepdims=True)
    )
    dscores_b = dscores.astype(bfloat)
    dqueries = (
        jnp.einsum("kgqp,pkd->qkgd", dscores_b, keys_back, preferred_element_type=single)
        * head_scale
    )
    dkeys = (
        jnp.einsum("kgqp,qkgd->pkd", dscores_b, grouped, preferred_element_type=single) * head_scale
    )
    dkeys_local, dvalues_local = (
        lax.psum_scatter(
            dkeys.reshape(seq_len, key_width).astype(jnp.bfloat16),
            "seq",
            scatter_dimension=0,
            tiled=True,
        ).astype(jnp.float32),
        lax.psum_scatter(
            d_values.reshape(seq_len, key_width).astype(jnp.bfloat16),
            "seq",
            scatter_dimension=0,
            tiled=True,
        ).astype(jnp.float32),
    )
    dquery_b = (
        rotate_back(dqueries.reshape(row_count, HEADS, HEAD_DIM), cosines, sines)
        .reshape(row_count, query_width)
        .astype(bfloat)
    )
    dkey_rot = rotate_back(
        dkeys_local.reshape(row_count, KV_HEADS, HEAD_DIM), cosines, sines
    ).reshape(row_count, key_width)
    dkeyval_b = jnp.concatenate([dkey_rot, dvalues_local], 1).astype(bfloat)
    d_query = jnp.dot(normed.T, dquery_b, preferred_element_type=single)
    d_keyval = jnp.dot(normed.T, dkeyval_b, preferred_element_type=single)
    dnormed = jnp.dot(dquery_b, query_b.T, preferred_element_type=single) + jnp.dot(
        dkeyval_b, keyval_b.T, preferred_element_type=single
    )
    dnorm_one, dgain_one = norm_back(inputs, scale_one, gains_f[0], dnormed)
    tokens_grad = dresidual + dnorm_one
    d_gains = jnp.stack([dgain_one, dgain_two])
    grad_query, grad_keyval, grad_output, grad_router, grad_gains = (
        lax.psum_scatter(d_query, ("dp", "seq"), scatter_dimension=0, tiled=True),
        lax.psum_scatter(d_keyval, ("dp", "seq"), scatter_dimension=0, tiled=True),
        lax.psum_scatter(d_output, ("dp", "seq"), scatter_dimension=0, tiled=True),
        lax.psum_scatter(d_router, ("dp", "seq"), scatter_dimension=0, tiled=True),
        lax.psum_scatter(d_gains, ("dp", "seq"), scatter_dimension=1, tiled=True),
    )
    grad_gateup, grad_down = (
        lax.psum_scatter(
            d_gateup.astype(jnp.bfloat16), "seq", scatter_dimension=1, tiled=True
        ).astype(jnp.float32),
        lax.psum_scatter(
            d_down.astype(jnp.bfloat16), "seq", scatter_dimension=1, tiled=True
        ).astype(jnp.float32),
    )
    base_rate = 0.5
    query_new = adamw(
        query_weight, grad_query, query_mean, query_square, base_rate * D ** (-0.5), 0.1
    )
    keyval_new = adamw(
        keyval_weight, grad_keyval, keyval_mean, keyval_square, base_rate * D ** (-0.5), 0.1
    )
    output_new = adamw(
        output_weight,
        grad_output,
        output_mean,
        output_square,
        base_rate * max(1, 2 * query_width // seq_len) ** (-0.5),
        0.1,
    )
    router_new = adamw(
        router_weight, grad_router, router_mean, router_square, base_rate * (4 * D) ** (-0.5), 0.1
    )
    gains_new = adamw(norm_gains, grad_gains, gains_mean, gains_square, 0.6, 0.0)
    gateup_new = adamw(
        gateup_weight, grad_gateup, gateup_mean, gateup_square, base_rate * D ** (-0.5), 0.1
    )
    down_new = adamw(
        down_weight, grad_down, down_mean, down_square, base_rate * (FF_E // 8) ** (-0.5), 0.1
    )
    return (
        layer_out,
        tokens_grad,
        query_new[0],
        query_new[1],
        query_new[2],
        keyval_new[0],
        keyval_new[1],
        keyval_new[2],
        output_new[0],
        output_new[1],
        output_new[2],
        router_new[0],
        router_new[1],
        router_new[2],
        gains_new[0],
        gains_new[1],
        gains_new[2],
        gateup_new[0],
        gateup_new[1],
        gateup_new[2],
        down_new[0],
        down_new[1],
        down_new[2],
    )


def solution(mesh):
    return jax.shard_map(
        body,
        mesh=mesh,
        in_specs=(
            P(("dp", "seq"), None),
            P(("dp", "seq"), None),
            P("dp"),
            P(("dp", "seq"), None),
            P(("dp", "seq"), None),
            P(("dp", "seq"), None),
            P(("dp", "seq"), None),
            P(("dp", "seq"), None),
            P(("dp", "seq"), None),
            P(("dp", "seq"), None),
            P(("dp", "seq"), None),
            P(("dp", "seq"), None),
            P(("dp", "seq"), None),
            P(("dp", "seq"), None),
            P(("dp", "seq"), None),
            P(("dp", "seq"), None),
            P(None, ("dp", "seq")),
            P(None, ("dp", "seq")),
            P(None, ("dp", "seq")),
            P("dp", "seq", None),
            P("dp", "seq", None),
            P("dp", "seq", None),
            P("dp", "seq", None),
            P("dp", "seq", None),
            P("dp", "seq", None),
        ),
        out_specs=(
            P(("dp", "seq"), None),
            P(("dp", "seq"), None),
            P(("dp", "seq"), None),
            P(("dp", "seq"), None),
            P(("dp", "seq"), None),
            P(("dp", "seq"), None),
            P(("dp", "seq"), None),
            P(("dp", "seq"), None),
            P(("dp", "seq"), None),
            P(("dp", "seq"), None),
            P(("dp", "seq"), None),
            P(("dp", "seq"), None),
            P(("dp", "seq"), None),
            P(("dp", "seq"), None),
            P(None, ("dp", "seq")),
            P(None, ("dp", "seq")),
            P(None, ("dp", "seq")),
            P("dp", "seq", None),
            P("dp", "seq", None),
            P("dp", "seq", None),
            P("dp", "seq", None),
            P("dp", "seq", None),
            P("dp", "seq", None),
        ),
        check_vma=False,
    )
```

profile of v0, /device:TPU:0, one launch (start us, length us, event | category | flops | bytes accessed | tf_op | source)
XLA Modules:
  0.0 3251.9 jit_solution(6368415607901930242)
XLA Ops:
  10.8 47.9 %all-gather = bf16[128,8,2]{1,2,0:T(2,128)(2,1)S(1)} all-gather(bf16[1,8,2]{1,2,0:T(2,128)(2,1)S(1)} %convert_bitcast_fusion.3), channel_id=1, replica_groups=mesh['dp'=32,'seq'=4] {'dp','seq'}, dimensions={0}, use_global_device_ids=true | all-gather | bytes 4128 | tf_op jit(solution)/shard_map/all_gather | solution.py:126
  61.5 17.9 all-gather.8.cloned.1.call-done
  108.0 37.6 %all-gather.12.cloned.1.call-done = bf16[1024,1024]{1,0:T(8,128)(2,1)} async-done(((bf16[8,1024]{1,0:T(8,128)(2,1)}), bf16[1024,1024]{1,0:T(8,128)(2,1)}) %all-gather.12.cloned.1.call-update) | async-done | bytes 2097168 | tf_op jit(solution)/shard_map/all_gather | solution.py:122
  148.6 27.8 all-gather.10.cloned.1.call-done
  205.4 39.6 %all-gather.14.cloned.1.call-done = bf16[1024,1024]{1,0:T(8,128)(2,1)} async-done(((bf16[8,1024]{1,0:T(8,128)(2,1)}), bf16[1024,1024]{1,0:T(8,128)(2,1)}) %all-gather.14.cloned.1.call-update) | async-done | bytes 2097168 | tf_op jit(solution)/shard_map/all_gather | solution.py:124
  248.6 14.0 gather_fusion
  276.5 31.8 all-gather.16.cloned.1.call-done
  308.3 46.1 %all-to-all-done = bf16[32,96,1024]{2,1,0:T(8,128)(2,1)} async-done(((bf16[32,96,1024]{2,1,0:T(8,128)(2,1)}), bf16[32,96,1024]{2,1,0:T(8,128)(2,1)}, u32[]{:S(2)}, u32[]{:S(2)}) %all-to-all-start) | async-done | bytes 6291488 | tf_op jit(solution)/shard_map/all_to_all | solution.py:186
  377.1 42.6 %copy.203 = bf16[1,3072,1024]{2,0,1:T(2,128)(2,1)} copy(bf16[1,3072,1024]{2,1,0:T(8,128)(2,1)S(1)} %convert_bitcast_fusion.1) | data formatting | bytes 12582912 | tf_op jit(solution)/shard_map/convert_element_type | solution.py:189
  420.2 38.1 %reduce = bf16[3072,1024]{1,0:T(8,128)(2,1)} reduce(bf16[3072,1,1024]{2,1,0:T(2,128)(2,1)} %bitcast.216, bf16[]{:T(256)} %broadcast.380), dimensions={1}, to_apply=%bitcast.204.reduce_sub_computation | reduce | bytes 12582914
  458.3 12.9 reshape.422
  471.2 12.8 all-to-all-start.1
  484.2 14.2 gather_fusion.3
  498.4 121.6 %all_gather.29 = bf16[1024,32]{1,0:T(8,128)(2,1)S(1)} all-gather(bf16[8,32]{1,0:T(8,128)(2,1)S(1)} %convert_element_type.178), channel_id=1, replica_groups=mesh['dp'=32,'seq'=4] {'dp','seq'}, dimensions={0}, use_global_device_ids=true | all-gather | bytes 66048 | tf_op jit(solution)/shard_map/all_gather | solution.py:125
  620.4 21.6 reshape.423
  651.8 14.5 gather_fusion.1
  671.2 17.4 gather_fusion.2
  695.3 79.1 %all_to_all.16 = bf16[32,96,1024]{2,1,0:T(8,128)(2,1)S(1)} all-to-all(bf16[32,96,1024]{2,1,0:T(8,128)(2,1)S(1)} %select_convert_fusion), channel_id=1, replica_groups=mesh['dp'=32,'seq'=4] {'dp'}, dimensions={0} | all-to-all | bytes 12582912 | tf_op jit(solution)/shard_map/all_to_all | solution.py:201
  791.6 42.6 %copy.202 = bf16[1,3072,1024]{2,0,1:T(2,128)(2,1)} copy(bf16[1,3072,1024]{2,1,0:T(8,128)(2,1)S(1)} %convert_bitcast_fusion) | data formatting | bytes 12582912 | tf_op jit(solution)/shard_map/convert_element_type | solution.py:216
  834.2 37.8 %reduce.1 = bf16[3072,1024]{1,0:T(8,128)(2,1)} reduce(bf16[3072,1,1024]{2,1,0:T(2,128)(2,1)} %bitcast.217, bf16[]{:T(256)} %broadcast.380), dimensions={1}, to_apply=%bitcast.203.reduce_sub_computation | reduce | bytes 12582914
  872.0 12.9 reshape.424
  895.9 73.2 %all-to-all-done.3 = bf16[32,2,49152]{2,1,0:T(2,128)(2,1)} async-done(((bf16[32,2,49152]{2,1,0:T(2,128)(2,1)}), bf16[32,2,49152]{2,1,0:T(2,128)(2,1)}, u32[]{:S(2)}, u32[]{:S(2)}) %all-to-all-start.3) | async-done | bytes 6291488 | tf_op jit(solution)/shard_map/all_to_all | solution.py:219
  969.0 21.7 reshape.425
  1000.6 14.9 gather_fusion.4
  1024.7 16.3 fusion
  1110.9 145.8 %all-reduce.4.cloned.1.call-done = f32[1024,32]{1,0:T(8,128)} async-done(((f32[1024,32]{1,0:T(8,128)}), f32[1024,32]{1,0:T(8,128)}) %all-reduce.4.cloned.1.call-update) | async-done | bytes 131088
  1258.0 24.7 reduce-scatter.21.cloned.1.call-done
  1285.5 29.0 reduce-scatter.19.cloned.1.call-done
  1321.4 65.7 %all-reduce.1 = f32[2,1024]{1,0:T(2,128)S(1)} all-reduce(f32[2,1024]{1,0:T(2,128)S(1)} %pad_maximum_fusion.13), channel_id=8, replica_groups=mesh['dp'=32,'seq'=4] {'dp','seq'}, use_global_device_ids=true, to_apply=%region_26.27.clone | all-reduce | flops 2048 | bytes 16384
  1391.0 570.1 %reduce-scatter.13.cloned.1.call-done = f32[8,1024]{1,0:T(8,128)} async-done(((f32[1024,1024]{1,0:T(8,128)}), f32[8,1024]{1,0:T(8,128)}) %reduce-scatter.13.cloned.1.call-update) | async-done | bytes 32784 | tf_op jit(solution)/shard_map/reduce_scatter | solution.py:287
  1962.5 639.8 %reduce-scatter.17.cloned.1.call-done = f32[8,1024]{1,0:T(8,128)} async-done(((f32[1024,1024]{1,0:T(8,128)}), f32[8,1024]{1,0:T(8,128)}) %reduce-scatter.17.cloned.1.call-update) | async-done | bytes 32784 | tf_op jit(solution)/shard_map/reduce_scatter | solution.py:289
  2603.7 639.8 %reduce-scatter.15.cloned.1.call-done = f32[8,1024]{1,0:T(8,128)} async-done(((f32[1024,1024]{1,0:T(8,128)}), f32[8,1024]{1,0:T(8,128)}) %reduce-scatter.15.cloned.1.call-update) | async-done | bytes 32784 | tf_op jit(solution)/shard_map/reduce_scatter | solution.py:288
  (305 shorter events, 263.7 us)
Async XLA Ops:
  7.2 72.2 %all-gather.8.cloned.1.call-start = ((), (), s32[]{:S(2)}) async-start(), calls=%async_computation.11 | async-start | bytes 2113536 | tf_op jit(solution)/shard_map/all_gather | solution.py:123
  8.6 137.0 %all-gather.12.cloned.1.call-start = ((), (), s32[]{:S(2)}) async-start(), calls=%async_computation.13 | async-start | bytes 2113536 | tf_op jit(solution)/shard_map/all_gather | solution.py:122
  10.1 166.4 %all-gather.10.cloned.1.call-start = ((), (), s32[]{:S(2)}) async-start(), calls=%async_computation.12 | async-start | bytes 2621440 | tf_op jit(solution)/shard_map/all_gather | solution.py:146
  85.2 159.8 %all-gather.14.cloned.1.call-start = ((), (), s32[]{:S(2)}) async-start(), calls=%async_computation.14 | async-start | bytes 2113536 | tf_op jit(solution)/shard_map/all_gather | solution.py:124
  248.6 371.4 %copy-start = (bf16[256,1024]{1,0:T(8,128)(2,1)}, bf16[256,1024]{1,0:T(8,128)(2,1)S(1)}, u32[]{:S(2)}) copy-start(bf16[256,1024]{1,0:T(8,128)(2,1)S(1)} %multiply_convert_fusion.1) | copy-start | bytes 1572868
  269.4 85.0 %all-to-all-start = ((bf16[32,96,1024]{2,1,0:T(8,128)(2,1)}), bf16[32,96,1024]{2,1,0:T(8,128)(2,1)}, u32[]{:S(2)}, u32[]{:S(2)}) async-start(bf16[32,96,1024]{2,1,0:T(8,128)(2,1)} %broadcast_select_fusion), calls=%async_computation | async-start | bytes 12582912 | tf_op jit(solution)/shard_map/all_to_all | solution.py:186
  274.5 33.7 %all-gather.16.cloned.1.call-start = ((), (), s32[]{:S(2)}) async-start(), calls=%async_computation.15 | async-start | bytes 2621440 | tf_op jit(solution)/shard_map/all_gather | solution.py:129
  275.5 96.0 %all-gather.18.cloned.1.call-start = ((), (), s32[]{:S(2)}) async-start(), calls=%async_computation.16 | async-start | bytes 1310720 | tf_op jit(solution)/shard_map/all_gather | solution.py:130
  471.2 149.2 %all-to-all-start.1 = ((bf16[32,2,49152]{2,1,0:T(2,128)(2,1)}), bf16[32,2,49152]{2,1,0:T(2,128)(2,1)}, u32[]{:S(2)}, u32[]{:S(2)}) async-start(bf16[32,2,49152]{2,1,0:T(2,128)(2,1)} %reshape.422), calls=%async_computation.1 | async-start | bytes 12582912 | tf_op jit(solution)/shard_map/all_to_all | solution.py:192
  484.2 135.8 %copy-start.55 = (s32[2048,1]{0,1:T(1,128)S(1)}, s32[2048,1]{0,1:T(1,128)}, u32[]{:S(2)}) copy-start(s32[2048,1]{0,1:T(1,128)} %copy-done.54) | copy-start | bytes 24580
  884.9 84.1 %all-to-all-start.3 = ((bf16[32,2,49152]{2,1,0:T(2,128)(2,1)}), bf16[32,2,49152]{2,1,0:T(2,128)(2,1)}, u32[]{:S(2)}, u32[]{:S(2)}) async-start(bf16[32,2,49152]{2,1,0:T(2,128)(2,1)} %reshape.424), calls=%async_computation.3 | async-start | bytes 12582912 | tf_op jit(solution)/shard_map/all_to_all | solution.py:219
  889.8 206.1 %reduce-scatter.9.cloned.1.call-start = ((), (), s32[]{:S(2)}) async-start(), calls=%async_computation.17 | async-start | bytes 1310720 | tf_op jit(solution)/shard_map/reduce_scatter | solution.py:256
  1052.5 54.5 %reduce-scatter.11.cloned.1.call-start = ((), (), s32[]{:S(2)}) async-start(), calls=%async_computation.18 | async-start | bytes 1310720 | tf_op jit(solution)/shard_map/reduce_scatter | solution.py:262
  1062.3 194.4 %all-reduce.4.cloned.1.call-start = ((), (), s32[]{:S(2)}) async-start(), calls=%async_computation.24 | async-start | bytes 1048576
  1063.5 219.1 %reduce-scatter.21.cloned.1.call-start = ((), (), s32[]{:S(2)}) async-start(), calls=%async_computation.23 | async-start | bytes 1310720 | tf_op jit(solution)/shard_map/reduce_scatter | solution.py:297
  1071.9 242.5 %reduce-scatter.19.cloned.1.call-start = ((), (), s32[]{:S(2)}) async-start(), calls=%async_computation.22 | async-start | bytes 2621440 | tf_op jit(solution)/shard_map/reduce_scatter | solution.py:294
  1083.9 877.2 %reduce-scatter.13.cloned.1.call-start = ((), (), s32[]{:S(2)}) async-start(), calls=%async_computation.19 | async-start | bytes 4227072 | tf_op jit(solution)/shard_map/reduce_scatter | solution.py:287
  1092.8 1509.6 %reduce-scatter.17.cloned.1.call-start = ((), (), s32[]{:S(2)}) async-start(), calls=%async_computation.21 | async-start | bytes 4227072 | tf_op jit(solution)/shard_map/reduce_scatter | solution.py:289
  1095.6 2147.9 %reduce-scatter.15.cloned.1.call-start = ((), (), s32[]{:S(2)}) async-start(), calls=%async_computation.20 | async-start | bytes 4227072 | tf_op jit(solution)/shard_map/reduce_scatter | solution.py:288
  1098.1 158.6 %copy-start.57 = (f32[8,32]{1,0:T(8,128)S(1)}, f32[8,32]{1,0:T(8,128)}, u32[]{:S(2)}) copy-start(f32[8,32]{1,0:T(8,128)} %param.38) | copy-start | bytes 3076
  1098.1 158.6 %copy-start.60 = (f32[8,32]{1,0:T(8,128)S(1)}, f32[8,32]{1,0:T(8,128)}, u32[]{:S(2)}) copy-start(f32[8,32]{1,0:T(8,128)} %param.39) | copy-start | bytes 3076
  1098.1 158.6 %copy-start.61 = (f32[8,32]{1,0:T(8,128)S(1)}, f32[8,32]{1,0:T(8,128)}, u32[]{:S(2)}) copy-start(f32[8,32]{1,0:T(8,128)} %param.40) | copy-start | bytes 3076
  1098.1 216.3 %copy-start.20 = (f32[1,256,1024]{2,1,0:T(8,128)S(1)}, f32[1,256,1024]{2,1,0:T(8,128)}, u32[]{:S(2)}) copy-start(f32[1,256,1024]{2,1,0:T(8,128)} %param.44) | copy-start | bytes 3145732
  1318.6 642.5 %copy-start.37 = (f32[8,1024]{1,0:T(8,128)S(1)}, f32[8,1024]{1,0:T(8,128)}, u32[]{:S(2)}) copy-start(f32[8,1024]{1,0:T(8,128)} %param.29) | copy-start | bytes 98308
  1318.6 642.5 %copy-start.48 = (f32[8,1024]{1,0:T(8,128)S(1)}, f32[8,1024]{1,0:T(8,128)}, u32[]{:S(2)}) copy-start(f32[8,1024]{1,0:T(8,128)} %param.30) | copy-start | bytes 98308
  1318.6 1283.7 %copy-start.38 = (f32[8,1024]{1,0:T(8,128)S(1)}, f32[8,1024]{1,0:T(8,128)}, u32[]{:S(2)}) copy-start(f32[8,1024]{1,0:T(8,128)} %param.35) | copy-start | bytes 98308
  1318.6 1924.9 %copy-start.39 = (f32[8,1024]{1,0:T(8,128)S(1)}, f32[8,1024]{1,0:T(8,128)}, u32[]{:S(2)}) copy-start(f32[8,1024]{1,0:T(8,128)} %param.32) | copy-start | bytes 98308
  1319.4 641.6 %copy-start.49 = (f32[8,1024]{1,0:T(8,128)S(1)}, f32[8,1024]{1,0:T(8,128)}, u32[]{:S(2)}) copy-start(f32[8,1024]{1,0:T(8,128)} %param.31) | copy-start | bytes 98308
  1319.4 1282.9 %copy-start.50 = (f32[8,1024]{1,0:T(8,128)S(1)}, f32[8,1024]{1,0:T(8,128)}, u32[]{:S(2)}) copy-start(f32[8,1024]{1,0:T(8,128)} %param.36) | copy-start | bytes 98308
  1319.4 1282.9 %copy-start.51 = (f32[8,1024]{1,0:T(8,128)S(1)}, f32[8,1024]{1,0:T(8,128)}, u32[]{:S(2)}) copy-start(f32[8,1024]{1,0:T(8,128)} %param.37) | copy-start | bytes 98308
  1319.5 1924.0 %copy-start.52 = (f32[8,1024]{1,0:T(8,128)S(1)}, f32[8,1024]{1,0:T(8,128)}, u32[]{:S(2)}) copy-start(f32[8,1024]{1,0:T(8,128)} %param.33) | copy-start | bytes 98308
  1319.5 1924.0 %copy-start.53 = (f32[8,1024]{1,0:T(8,128)S(1)}, f32[8,1024]{1,0:T(8,128)}, u32[]{:S(2)}) copy-start(f32[8,1024]{1,0:T(8,128)} %param.34) | copy-start | bytes 98308
  (57 other events, 1511.6 us)
Sparse Core Ops, SparseCore 0:
  11.6 67.7 all-gather.7
  82.9 62.6 all-gather.11
  147.9 28.4 all-gather.9
  179.8 65.1 all-gather.13
  277.3 30.9 all-gather.15
  310.3 24.0 all-gather.17
  1052.6 27.9 reduce-scatter.8
  1083.7 23.2 reduce-scatter.10
  1112.4 144.2 all-reduce.3
  1259.6 22.9 reduce-scatter.20
  1285.0 29.3 reduce-scatter.18
  1316.8 644.2 reduce-scatter.12
  1963.4 638.8 reduce-scatter.16
  2604.6 638.8 reduce-scatter.14
where the time goes:
time: 3260 us; the launch traced here: 3250 us
  waiting for transfers between devices  2330 us (71%)
  blocking collectives  314 us (10%)
  local copies, waits for them, and re-layouts  275 us (8%)
  other arithmetic  160 us (5%)
  matrix products  129 us (4%)
    reduce_scatter x1, waiting for transfers between devices, body(): lax.psum_scatter(d_output, ('dp', 'seq'), scatter_dimension=0, tiled=True)  640 us
    reduce_scatter x1, waiting for transfers between devices, body(): lax.psum_scatter(d_keyval, ('dp', 'seq'), scatter_dimension=0, tiled=True)  640 us
    reduce_scatter x1, waiting for transfers between devices, body(): lax.psum_scatter(d_query, ('dp', 'seq'), scatter_dimension=0, tiled=True)  570 us
    unnamed x15, waiting for transfers between devices  146 us
    all_gather x1, blocking collectives, body(): lax.all_gather(router_weight.astype(bfloat), ('dp', 'seq'), axis=0, tiled...  122 us
    unnamed x152, local copies, waits for them, and re-layouts  95.8 us
    all_to_all x1, blocking collectives, body(): lax.all_to_all(slot_grads, 'dp', split_axis=0, concat_axis=1, tiled=True)  79.1 us
    unnamed x5, other arithmetic  76.6 us
  transfers between devices with their start and end apart: 17, of which 14 were waited for; matrix products, arithmetic and copies ran while one was open for 5% of the time, Pallas kernels for 0%

commit v1 on v0

v1 whole, which is shorter than its diff:
```python
import jax
import jax.numpy as jnp
from jax import lax
from jax.experimental import pallas as pl
from jax.experimental.pallas import tpu as pltpu
from jax.sharding import PartitionSpec as P

MESH = pl.DeviceIdType.MESH
bf16 = jnp.bfloat16
f32 = jnp.float32
AXES = "xycz"


def place():
    dp = lax.axis_index("dp")
    return {"x": dp // 8, "y": (dp // 2) % 4, "c": dp % 2, "z": lax.axis_index("seq")}


def device(at):
    return ((at["x"] * 4 + at["y"]) * 2 + at["c"], at["z"])


def shift(at, axis, by):
    size = 2 if axis == "c" else 4
    return lax.rem(at[axis] + by, size)


def peer(at, axis, by):
    return device({**at, axis: shift(at, axis, by)})


def greet(at, axes):
    barrier = pltpu.get_barrier_semaphore()
    count = 0
    for axis in axes:
        for by in (1,) if axis == "c" else (1, 2, 3):
            pl.semaphore_signal(
                barrier, inc=1, device_id=peer(at, axis, by), device_id_type=MESH
            )
            count += 1
    pl.semaphore_wait(barrier, count)


class Wires:
    def __init__(self, send_sems, recv_sems, local_sems=None):
        self.send_sems, self.recv_sems, self.local_sems = send_sems, recv_sems, local_sems
        self.copies, self.local = [], 0

    def send(self, src, dst, target):
        at = len(self.copies)
        copy = pltpu.make_async_remote_copy(
            src_ref=src,
            dst_ref=dst,
            send_sem=self.send_sems.at[at],
            recv_sem=self.recv_sems.at[at],
            device_id=target,
            device_id_type=MESH,
        )
        copy.start()
        self.copies.append(copy)
        return copy

    def keep(self, src, dst):
        copy = pltpu.make_async_copy(src, dst, self.local_sems.at[self.local])
        copy.start()
        self.local += 1
        return copy

    def finish(self):
        for copy in self.copies:
            copy.wait_send()


def index(at, whole, **fixed):
    spots = {**at, **fixed}
    return tuple(slice(None) if axis in whole else spots[axis] for axis in AXES)


GATHER_ORDERS = ("zyx", "xzy", "yxz")


def gather_front_kernel(
    wq, wkv, wo, tok, oq, okv, oo, ot, send_sems, recv_sems, local_sems
):
    at = place()
    wires = Wires(send_sems, recv_sems, local_sems)
    parts = list(zip((wq, wkv, wo), (oq, okv, oo), GATHER_ORDERS))
    kept = [wires.keep(w, o.at[index(at, "")]) for w, o, _ in parts]
    kept.append(wires.keep(tok, ot.at[at["z"]]))
    greet(at, "xyzc")
    arrivals = {}
    for p, (w, o, order) in enumerate(parts):
        for by in (1, 3, 2):
            arrivals[p, by] = wires.send(w, o.at[index(at, "")], peer(at, order[0], by))
    half = tok.shape[0] // 2
    low, high = pl.ds(0, half), pl.ds(half, half)
    z = at["z"]
    from_left = wires.send(tok, ot.at[z], peer(at, "z", 1))
    from_right = wires.send(tok, ot.at[z], peer(at, "z", 3))
    for copy in kept:
        copy.wait()
    for stage in (1, 2):
        later = {}
        for p, (w, o, order) in enumerate(parts):
            for by in (1, 3, 2):
                arrivals[p, by].wait_recv()
            spot = index(at, order[:stage])
            for by in (1, 3, 2):
                later[p, by] = wires.send(o.at[spot], o.at[spot], peer(at, order[stage], by))
        arrivals = later
    sibling = peer(at, "c", 1)
    across = []
    for p, (w, o, order) in enumerate(parts):
        spot = index(at, order[:2])
        across.append(wires.send(o.at[spot], o.at[spot], sibling))
    from_left.wait_recv()
    left, right = shift(at, "z", 3), shift(at, "z", 1)
    far = [wires.send(ot.at[left, low], ot.at[left, low], peer(at, "z", 1))]
    from_right.wait_recv()
    far.append(wires.send(ot.at[right, high], ot.at[right, high], peer(at, "z", 3)))
    for by in (1, 3, 2):
        for p, (w, o, order) in enumerate(parts):
            arrivals[p, by].wait_recv()
            spot = index(at, order[:2], **{order[2]: shift(at, order[2], 4 - by)})
            across.append(wires.send(o.at[spot], o.at[spot], sibling))
    for copy in far + across:
        copy.wait_recv()
    wires.finish()


def gather_front(wq, wkv, wo, tok):
    shapes = [pltpu.HBM((4, 4, 2, 4) + w.shape, w.dtype) for w in (wq, wkv, wo)]
    shapes.append(pltpu.HBM((4,) + tok.shape, tok.dtype))
    count = 9 * 3 + 4 + 12
    return pl.pallas_call(
        gather_front_kernel,
        out_shape=shapes,
        in_specs=[pl.BlockSpec(memory_space=pltpu.HBM)] * 4,
        out_specs=[pl.BlockSpec(memory_space=pltpu.HBM)] * 4,
        scratch_shapes=[
            pltpu.SemaphoreType.DMA((count,)),
            pltpu.SemaphoreType.DMA((count,)),
            pltpu.SemaphoreType.DMA((4,)),
        ],
        compiler_params=pltpu.CompilerParams(collective_id=1, has_side_effects=True),
        name="gather_front",
    )(*(pltpu.with_memory_space_constraint(v, pltpu.HBM) for v in (wq, wkv, wo, tok)))


PLANE_ORDERS = ("xy", "yx")


def gather_plane_kernel(n, o, send_sems, recv_sems, local_sems):
    at = place()
    wires = Wires(send_sems, recv_sems, local_sems)
    half = n.shape[0] // 2
    rows = [pl.ds(0, half), pl.ds(half, half)]

    def spot(h, **fixed):
        where = {**at, **fixed}
        return o.at[where["x"], where["y"], where["c"], rows[h]]

    mine = o.at[at["x"], at["y"], at["c"]]
    kept = wires.keep(n, mine)
    greet(at, "xyc")
    sibling = peer(at, "c", 1)
    first, second, across = {}, {}, []
    for by in (1, 3, 2):
        for h in (0, 1):
            axis = PLANE_ORDERS[h][0]
            first[h, by] = wires.send(n.at[rows[h]], spot(h), peer(at, axis, by))
    for h in (0, 1):
        axis = PLANE_ORDERS[h][1]
        for to in (1, 3):
            second[h, 0, to] = wires.send(n.at[rows[h]], spot(h), peer(at, axis, to))
    across.append(wires.send(n, mine, sibling))
    for by in (1, 3, 2):
        for h in (0, 1):
            one, two = PLANE_ORDERS[h]
            first[h, by].wait_recv()
            unit = spot(h, **{one: shift(at, one, 4 - by)})
            for to in (1, 3):
                second[h, by, to] = wires.send(unit, unit, peer(at, two, to))
            across.append(wires.send(unit, unit, sibling))
    far = []
    for by in (0, 1, 3, 2):
        for h in (0, 1):
            one, two = PLANE_ORDERS[h]
            for to in (1, 3):
                second[h, by, to].wait_recv()
                unit = spot(
                    h, **{one: shift(at, one, (4 - by) % 4), two: shift(at, two, 4 - to)}
                )
                if (to == 1) == (by in (0, 3)):
                    far.append(((h, by, to), wires.send(unit, unit, peer(at, two, to))))
                across.append(wires.send(unit, unit, sibling))
    for (h, by, to), copy in far:
        one, two = PLANE_ORDERS[h]
        copy.wait_recv()
        unit = spot(h, **{one: shift(at, one, (4 - by) % 4), two: shift(at, two, 2)})
        across.append(wires.send(unit, unit, sibling))
    for copy in across:
        copy.wait_recv()
    kept.wait()
    wires.finish()


def gather_plane(n, collective_id):
    count = 6 + 16 + 8 + 31
    return pl.pallas_call(
        gather_plane_kernel,
        out_shape=pltpu.HBM((4, 4, 2) + n.shape, n.dtype),
        in_specs=[pl.BlockSpec(memory_space=pltpu.HBM)],
        out_specs=pl.BlockSpec(memory_space=pltpu.HBM),
        scratch_shapes=[
            pltpu.SemaphoreType.DMA((count,)),
            pltpu.SemaphoreType.DMA((count,)),
            pltpu.SemaphoreType.DMA((1,)),
        ],
        compiler_params=pltpu.CompilerParams(
            collective_id=collective_id, has_side_effects=True
        ),
        name="gather_plane",
    )(pltpu.with_memory_space_constraint(n, pltpu.HBM))


STRIP = 16


def add_rows(out, parts, rows):
    def strip(i, carry):
        span = pl.ds(pl.multiple_of(i * STRIP, STRIP), STRIP)
        total = parts[0][span].astype(f32)
        for part in parts[1:]:
            total = total + part[span].astype(f32)
        out[span] = total.astype(out.dtype)
        return carry

    lax.fori_loop(0, rows // STRIP, strip, 0)


def sum_plane_kernel(
    c_ref, out, held, crossed, near, mid, last, send_sems, recv_sems, local_sems
):
    at = place()
    wires = Wires(send_sems, recv_sems, local_sems)
    whole = out.shape[0]
    half = whole // 2
    rows = [pl.ds(0, half), pl.ds(half, half)]
    orders = ("yx", "xy")
    blocks = [(2, 2), (0, 2), (2, 0), (1, 2), (2, 1), (3, 2), (2, 3)]
    blocks += [(0, 1), (1, 0), (0, 3), (3, 0), (1, 1), (3, 3), (1, 3), (3, 1), (0, 0)]
    other = shift(at, "c", 1)

    def spot(dx, dy):
        return shift(at, "x", dx), shift(at, "y", dy)

    kept = [
        wires.keep(c_ref.at[spot(*b) + (at["c"],)], held.at[spot(*b)]) for b in blocks
    ]
    greet(at, "xyc")
    sibling = peer(at, "c", 1)
    crossing = {}
    for b in blocks:
        crossing[b] = wires.send(
            c_ref.at[spot(*b) + (other,)], crossed.at[spot(*b)], sibling
        )

    def unit(h, d1, d2):
        dx, dy = (d2, d1) if h == 0 else (d1, d2)
        return held.at[spot(dx, dy) + (rows[h],)]

    step1, step2 = {}, {}

    def settle(b, number):
        kept[number].wait()
        crossing[b].wait_recv()
        add_rows(held.at[spot(*b)], [held.at[spot(*b)], crossed.at[spot(*b)]], whole)

    for number, b in enumerate(blocks):
        settle(b, number)
        for h in (0, 1):
            d1, d2 = (b[1], b[0]) if h == 0 else (b[0], b[1])
            axis = orders[h][0]
            if d1 == 2:
                to = 1 if d2 < 2 else 3
                step1[h, d2] = wires.send(
                    unit(h, 2, d2), near.at[h, d2], peer(at, axis, to)
                )
            elif (d1 == 1 and d2 >= 2) or (d1 == 3 and d2 < 2):
                step2[h, d1, d2] = wires.send(
                    unit(h, d1, d2), mid.at[h, d1 // 2, d2], peer(at, axis, d1)
                )
    for d2 in (0, 2, 1, 3):
        for h in (0, 1):
            d1 = 1 if d2 < 2 else 3
            axis = orders[h][0]
            step1[h, d2].wait_recv()
            add_rows(unit(h, d1, d2), [unit(h, d1, d2), near.at[h, d2]], half)
            step2[h, d1, d2] = wires.send(
                unit(h, d1, d2), mid.at[h, d1 // 2, d2], peer(at, axis, d1)
            )
    ends = {}
    for d2 in (2, 1, 3, 0):
        for h in (0, 1):
            for d1 in (1, 3):
                step2[h, d1, d2].wait_recv()
            add_rows(
                unit(h, 0, d2), [unit(h, 0, d2), mid.at[h, 0, d2], mid.at[h, 1, d2]], half
            )
            if d2:
                ends[h, d2] = wires.send(
                    unit(h, 0, d2), last.at[h, d2 - 1], peer(at, orders[h][1], d2)
                )
    for h in (0, 1):
        for d2 in (1, 3, 2):
            ends[h, d2].wait_recv()
        add_rows(
            out.at[rows[h]],
            [unit(h, 0, 0), last.at[h, 0], last.at[h, 1], last.at[h, 2]],
            half,
        )
    wires.finish()


def sum_plane(c, collective_id, dtype):
    rows, width = c.shape[-2:]
    half = rows // 2
    count = 16 + 8 + 16 + 6
    return pl.pallas_call(
        sum_plane_kernel,
        out_shape=jax.ShapeDtypeStruct((rows, width), dtype),
        in_specs=[pl.BlockSpec(memory_space=pltpu.HBM)],
        out_specs=pl.BlockSpec(memory_space=pltpu.VMEM),
        scratch_shapes=[
            pltpu.VMEM((4, 4, rows, width), bf16),
            pltpu.VMEM((4, 4, rows, width), bf16),
            pltpu.VMEM((2, 4, half, width), bf16),
            pltpu.VMEM((2, 2, 4, half, width), bf16),
            pltpu.VMEM((2, 3, half, width), bf16),
            pltpu.SemaphoreType.DMA((count,)),
            pltpu.SemaphoreType.DMA((count,)),
            pltpu.SemaphoreType.DMA((16,)),
        ],
        compiler_params=pltpu.CompilerParams(
            collective_id=collective_id,
            has_side_effects=True,
            vmem_limit_bytes=56 * 1024 * 1024,
        ),
        name="sum_plane",
    )(pltpu.with_memory_space_constraint(c, pltpu.HBM))


SUM_ORDERS = ("xyz", "yzx", "zxy")


def pick(ref, axes, axis, mine):
    return ref.at[tuple(mine if a == axis else slice(None) for a in axes)]


def sum_back_kernel(*refs):
    mats, dn1 = refs[0:3], refs[3]
    outs, dn1_out = refs[4:7], refs[7]
    scratch = refs[8:-3]
    send_sems, recv_sems, local_sems = refs[-3:]
    crossed, held, one, two, three, sum1, sum2 = [scratch[i * 3 : i * 3 + 3] for i in range(7)]
    zmid, zlast, znear = scratch[21:24]
    at = place()
    wires = Wires(send_sems, recv_sems, local_sems)
    greet(at, "xyzc")
    sibling = peer(at, "c", 1)
    other = shift(at, "c", 1)
    crossing = [
        wires.send(mats[p].at[:, :, other], crossed[p], sibling) for p in range(3)
    ]
    half = dn1.shape[1] // 2
    low, high = pl.ds(0, half), pl.ds(half, half)
    z = at["z"]
    ahead, back, far = shift(at, "z", 1), shift(at, "z", 3), shift(at, "z", 2)
    up, down = peer(at, "z", 1), peer(at, "z", 3)
    znear_l = wires.send(dn1.at[far, low], znear.at[0], up)
    znear_r = wires.send(dn1.at[far, high], znear.at[1], down)
    zpure_l = wires.send(dn1.at[ahead, high], zlast.at[0, high], up)
    zpure_r = wires.send(dn1.at[back, low], zlast.at[1, low], down)

    def total(out, parts, count):
        def body(i, carry):
            value = parts[0][i].astype(f32)
            for part in parts[1:]:
                value = value + part[i].astype(f32)
            out[i] = value.astype(out.dtype)
            return carry

        lax.fori_loop(0, count, body, 0)

    stage1 = {}
    for p in range(3):
        crossing[p].wait_recv()

        def body(i, carry, p=p):
            mine = mats[p][i // 4, i % 4, at["c"]]
            held[p][i // 4, i % 4] = (
                mine.astype(f32) + crossed[p][i // 4, i % 4].astype(f32)
            ).astype(bf16)
            return carry

        lax.fori_loop(0, 16, body, 0)
        axis = SUM_ORDERS[p][0]
        for by in (2, 1, 3):
            stage1[p, by] = wires.send(
                pick(held[p], "xyz", axis, shift(at, axis, by)),
                one[p].at[by - 1],
                peer(at, axis, by),
            )
    znear_l.wait_recv()
    add_rows(zmid.at[0], [dn1.at[ahead, low], znear.at[0]], half)
    zsum_l = wires.send(zmid.at[0], zlast.at[0, low], up)
    znear_r.wait_recv()
    add_rows(zmid.at[1], [dn1.at[back, high], znear.at[1]], half)
    zsum_r = wires.send(zmid.at[1], zlast.at[1, high], down)
    stage2 = {}
    for p in range(3):
        axis, after = SUM_ORDERS[p][0], SUM_ORDERS[p][1]
        rest = "xyz".replace(axis, "")
        for by in (1, 3, 2):
            stage1[p, by].wait_recv()
        total(
            sum1[p],
            [pick(held[p], "xyz", axis, at[axis])] + [one[p].at[k] for k in range(3)],
            4,
        )
        for by in (2, 1, 3):
            stage2[p, by] = wires.send(
                pick(sum1[p], rest, after, shift(at, after, by)),
                two[p].at[by - 1],
                peer(at, after, by),
            )
    stage3 = {}
    for p in range(3):
        axis, after, end = SUM_ORDERS[p]
        rest = "xyz".replace(axis, "")
        for by in (1, 3, 2):
            stage2[p, by].wait_recv()
        total(
            sum2[p],
            [pick(sum1[p], rest, after, at[after])] + [two[p].at[k] for k in range(3)],
            4,
        )
        for by in (2, 1, 3):
            stage3[p, by] = wires.send(
                sum2[p].at[shift(at, end, by)], three[p].at[by - 1], peer(at, end, by)
            )
    for copy in (zpure_l, zsum_l, zpure_r, zsum_r):
        copy.wait_recv()
    add_rows(dn1_out, [dn1.at[z], zlast.at[0], zlast.at[1]], 2 * half)
    for p in range(3):
        for by in (1, 3, 2):
            stage3[p, by].wait_recv()
        value = sum2[p][at[SUM_ORDERS[p][2]]].astype(f32)
        for k in range(3):
            value = value + three[p][k].astype(f32)
        outs[p][...] = value
    wires.finish()


def sum_back(mats, dn1):
    widths = [m.shape[-1] for m in mats]
    rows, model = dn1.shape[1:]
    count = 3 * 10 + 6
    scratch = []
    for lead in ((4, 4, 4), (4, 4, 4), (3, 4, 4), (3, 4), (3,), (4, 4), (4,)):
        scratch += [pltpu.VMEM(lead + (16, w), bf16) for w in widths]
    scratch += [
        pltpu.VMEM((2, rows // 2, model), bf16),
        pltpu.VMEM((2, rows, model), bf16),
        pltpu.VMEM((2, rows // 2, model), bf16),
        pltpu.SemaphoreType.DMA((count,)),
        pltpu.SemaphoreType.DMA((count,)),
        pltpu.SemaphoreType.DMA((1,)),
    ]
    vmem = pl.BlockSpec(memory_space=pltpu.VMEM)
    return pl.pallas_call(
        sum_back_kernel,
        out_shape=[jax.ShapeDtypeStruct((16, w), f32) for w in widths]
        + [jax.ShapeDtypeStruct((rows, model), f32)],
        in_specs=[vmem] * 4,
        out_specs=[vmem] * 4,
        scratch_shapes=scratch,
        compiler_params=pltpu.CompilerParams(
            collective_id=4, has_side_effects=True, vmem_limit_bytes=56 * 1024 * 1024
        ),
        name="sum_back",
    )(*mats, dn1)


D = 1024
HEADS = 16
KV_HEADS = 8
HEAD_DIM = 64
EXPERTS = 32
FF_E = 512
STEP = 10
CAP = 96
TOK = 256


norm_epsilon = 1e-06
beta_first = 0.9
beta_second = 0.95
adam_epsilon = 1e-08
masked_score = -1e30


def rotary_tables(positions, half_width):
    freqs = 10000.0 ** (-jnp.arange(half_width, dtype=jnp.float32) / half_width)
    angles = positions.astype(jnp.float32)[:, None] * freqs[None, :]
    cosines = jnp.cos(angles)
    sines = jnp.sin(angles)
    return (jnp.concatenate([cosines, cosines], 1), jnp.concatenate([sines, sines], 1))


def rotate(values, cosines, sines):
    half_width = values.shape[-1] // 2
    turned = jnp.concatenate([-values[..., half_width:], values[..., :half_width]], -1)
    return values * cosines[:, None, :] + turned * sines[:, None, :]


def rotate_back(grads, cosines, sines):
    half_width = grads.shape[-1] // 2
    scaled = grads * sines[:, None, :]
    return grads * cosines[:, None, :] + jnp.concatenate(
        [scaled[..., half_width:], -scaled[..., :half_width]], -1
    )


def rms_scale(values):
    return lax.rsqrt(jnp.mean(values * values, axis=-1, keepdims=True) + norm_epsilon)


def norm_back(values, scale, gain, dnormed):
    scaled = values * scale
    dgain = jnp.sum(dnormed * scaled, axis=0)
    dscaled = dnormed * gain
    dvalues = scale * (dscaled - scaled * jnp.mean(dscaled * scaled, axis=-1, keepdims=True))
    return (dvalues, dgain)


def masked_scores(grouped, whole_kv, positions, length):
    key_count = whole_kv.shape[0]
    key_width = whole_kv.shape[1] // 2
    heads_kv = grouped.shape[1]
    head_size = grouped.shape[3]
    all_keys = whole_kv[:, :key_width].reshape(key_count, heads_kv, head_size)
    all_values = whole_kv[:, key_width:].reshape(key_count, heads_kv, head_size)
    raw_scores = jnp.einsum(
        "qkgd,pkd->kgqp", grouped, all_keys, preferred_element_type=jnp.float32
    ) * head_size ** (-0.5)
    key_pos = jnp.arange(key_count, dtype=jnp.int32)
    allowed = (key_pos[None, :] <= positions[:, None]) & (key_pos[None, :] < length)
    return (jnp.where(allowed, raw_scores, masked_score), all_keys, all_values)


def adamw(weight, grad, first, second, rate, decay):
    first_new = beta_first * first + (1.0 - beta_first) * grad
    second_new = beta_second * second + (1.0 - beta_second) * grad * grad
    update = (
        first_new
        / (1.0 - beta_first**STEP)
        / (jnp.sqrt(second_new / (1.0 - beta_second**STEP)) + adam_epsilon)
    )
    return (weight - rate * (update + decay * weight), first_new, second_new)


GROUP = 4


def matmul(a, b, contract):
    return lax.dot_general(
        a, b, (((contract[0],), (contract[1],)), ((), ())), preferred_element_type=f32
    )


def expert_kernel(n_ref, g_ref, w_ref, dn_ref, out_ref, dw_ref, xs, ds, dzs, gys, acc_gu, acc_d):
    step = pl.program_id(0)
    expert = lax.axis_index("dp")

    @pl.when(step == 0)
    def _():
        acc_gu[...] = jnp.zeros_like(acc_gu)
        acc_d[...] = jnp.zeros_like(acc_d)

    lane8 = lax.broadcasted_iota(jnp.int32, (8, 128), 1)
    sub8 = lax.broadcasted_iota(jnp.int32, (8, 128), 0)
    choose = (lane8 == expert + EXPERTS * sub8).astype(f32).astype(bf16)
    slot_row = lax.broadcasted_iota(jnp.int32, (CAP, TOK), 0).astype(f32)
    gates = []
    for b in range(GROUP):
        meta = n_ref[b, :, D:]
        fields = matmul(choose, meta, (1, 1))
        hot = slot_row == fields[0:1]
        pick_rows = jnp.where(hot, 1.0, 0.0).astype(bf16)
        gate_row = fields[1:2] + fields[2:3]
        gates.append(jnp.sum(jnp.where(hot, gate_row, 0.0), axis=1, keepdims=True))
        span = pl.ds(b * CAP, CAP)
        xs[span, :] = matmul(pick_rows, n_ref[b, :, :D], (1, 0)).astype(bf16)
        ds[span, :] = matmul(pick_rows, g_ref[b], (1, 0)).astype(bf16)
    gate = jnp.concatenate(gates, axis=0)
    w_gu = w_ref[:, : D // 4, :].reshape(D, 2 * FF_E)
    w_d = w_ref[:, D // 4 :, :].reshape(FF_E, D)
    x = xs[...]
    gu = matmul(x, w_gu, (1, 0))
    g_part, u_part = gu[:, :FF_E], gu[:, FF_E:]
    sig = 1.0 / (1.0 + jnp.exp(-g_part))
    act = g_part * sig
    hid = (act * u_part).astype(bf16)
    y = matmul(hid, w_d, (1, 0)).astype(bf16).astype(f32)
    dout = ds[...].astype(f32)
    dgate = jnp.sum(y * dout, axis=1, keepdims=True)
    gys[...] = (gate * y).astype(bf16)
    dy = (gate * dout).astype(bf16)
    dh = matmul(dy, w_d, (1, 1))
    da_g = dh * u_part * (sig * (1.0 + g_part * (1.0 - sig)))
    da = jnp.concatenate([da_g, dh * act], axis=1).astype(bf16)
    acc_d[...] += matmul(hid, dy, (0, 0))
    acc_gu[...] += matmul(x, da, (0, 0))
    dzs[:, :D] = matmul(da, w_gu, (1, 1)).astype(bf16)
    lane = lax.broadcasted_iota(jnp.int32, (GROUP * CAP, 128), 1)
    high = dgate.astype(bf16).astype(f32)
    fields = jnp.where(lane == expert, high, jnp.where(lane == expert + EXPERTS, dgate - high, 0.0))
    dzs[:, D:] = fields.astype(bf16)
    slot_lane = lax.broadcasted_iota(jnp.int32, (TOK, CAP), 1).astype(f32)
    lane_t = lax.broadcasted_iota(jnp.int32, (TOK, 128), 1)
    for b in range(GROUP):
        meta = n_ref[b, :, D:].astype(f32)
        rank = jnp.sum(jnp.where(lane_t == expert, meta, 0.0), axis=1, keepdims=True)
        spread = jnp.where(slot_lane == rank, 1.0, 0.0).astype(bf16)
        span = pl.ds(b * CAP, CAP)
        dn_ref[b] = matmul(spread, dzs[span, :], (1, 0)).astype(bf16)
        out_ref[b] = matmul(spread, gys[span, :], (1, 0)).astype(bf16)

    @pl.when(step == pl.num_programs(0) - 1)
    def _():
        dw_ref[:, : D // 4, :] = acc_gu[...].astype(bf16).reshape(4, D // 4, 2 * FF_E)
        dw_ref[:, D // 4 :, :] = acc_d[...].astype(bf16).reshape(4, FF_E // 4, D)


def experts(n_all, g_all, weights):
    sources = n_all.shape[0]
    wide = n_all.shape[2]
    rows = GROUP * CAP

    def block(width):
        return pl.BlockSpec((GROUP, TOK, width), lambda i: (i, 0, 0))

    def fixed(shape):
        return pl.BlockSpec(shape, lambda i: (0, 0, 0), pipeline_mode=pl.Buffered(1))

    return pl.pallas_call(
        expert_kernel,
        grid=(sources // GROUP,),
        out_shape=[
            jax.ShapeDtypeStruct(n_all.shape, bf16),
            jax.ShapeDtypeStruct(g_all.shape, bf16),
            jax.ShapeDtypeStruct(weights.shape, bf16),
        ],
        in_specs=[block(wide), block(D), fixed(weights.shape)],
        out_specs=[block(wide), block(D), fixed(weights.shape)],
        scratch_shapes=[
            pltpu.VMEM((rows, D), bf16),
            pltpu.VMEM((rows, D), bf16),
            pltpu.VMEM((rows, wide), bf16),
            pltpu.VMEM((rows, D), bf16),
            pltpu.VMEM((D, 2 * FF_E), f32),
            pltpu.VMEM((FF_E, D), f32),
        ],
        compiler_params=pltpu.CompilerParams(
            dimension_semantics=("arbitrary",), vmem_limit_bytes=58 * 1024 * 1024
        ),
        cost_estimate=pl.CostEstimate(
            flops=sources * CAP * D * FF_E * 18, bytes_accessed=75_000_000, transcendentals=0
        ),
        name="experts",
    )(n_all, g_all, weights)


def turned_rows(u, cos, sin, back):
    lane = lax.broadcasted_iota(jnp.int32, (1, 128), 1)
    first = lax.rem(lane, HEAD_DIM) < HEAD_DIM // 2
    pieces = []
    for j in range(u.shape[1] // 128):
        v = u[:, j * 128 : (j + 1) * 128]
        w = v * sin if back else v
        ahead = pltpu.roll(w, 128 - HEAD_DIM // 2, 1)
        behind = pltpu.roll(w, HEAD_DIM // 2, 1)
        if back:
            pieces.append(v * cos + jnp.where(first, ahead, -behind))
        else:
            pieces.append(v * cos + jnp.where(first, -ahead, behind) * sin)
    return jnp.concatenate(pieces, axis=1)


def unpack_into(out, packed):
    def chunk(i, carry):
        x = packed[pl.ds(i * 16, 16), :, :512].astype(f32)
        rows = pl.ds(pl.multiple_of(i * 128, 128), 128)
        out[rows, :512] = x[:, :8].reshape(128, 512).astype(bf16)
        out[rows, 512:] = x[:, 8:].reshape(128, 512).astype(bf16)
        return carry

    lax.fori_loop(0, 8, chunk, 0)


def gain_rows(small):
    lane = lax.broadcasted_iota(jnp.int32, (8, 128), 1)
    sub = lax.broadcasted_iota(jnp.int32, (8, 128), 0)
    choose = (lane == EXPERTS + sub).astype(f32).astype(bf16)
    return matmul(choose, small, (1, 1))


def fill_bias(bias, length, first_row):
    rows = lax.broadcasted_iota(jnp.int32, bias.shape, 0) + first_row
    keys = lax.broadcasted_iota(jnp.int32, bias.shape, 1)
    bias[...] = jnp.where((keys <= rows) & (keys < length), 0.0, masked_score)


def front_kernel(
    length, wq_p, wkv_p, wo_p, tok, routes, cos, sin,
    n_out, n1_out, q_out, kv_out, lse_out, ho_out, r_out, gate_out, wq, wkv, wo, small_out,
    bias,
):
    z = lax.axis_index("seq")
    unpack_into(wkv, wkv_p)
    unpack_into(wq, wq_p)

    def small_chunk(i, carry):
        x = wo_p[pl.ds(i * 16, 16), :, 512:].astype(f32)
        rows = pl.ds(pl.multiple_of(i * 128, 128), 128)
        small_out[rows, :] = x[:, :8].reshape(128, 128).astype(bf16)
        return carry

    lax.fori_loop(0, 8, small_chunk, 0)
    unpack_into(wo, wo_p)
    gains = gain_rows(small_out[...])
    fill_bias(bias, length[0], z * TOK)
    width = KV_HEADS * HEAD_DIM

    def block(b, carry):
        x = tok[b].astype(f32)
        n1 = (x * rms_scale(x) * gains[0:1]).astype(bf16)
        rows = pl.ds(pl.multiple_of(b * TOK, TOK), TOK)
        n1_out[rows, :] = n1
        kv = matmul(n1, wkv[...], (1, 0))
        kv_out[rows, :width] = turned_rows(
            kv[:, :width], cos[rows, :], sin[rows, :], False
        ).astype(bf16)
        kv_out[rows, width:] = kv[:, width:].astype(bf16)
        return carry

    lax.fori_loop(0, 4, block, 0)
    own = pl.ds(pl.multiple_of(z * TOK, TOK), TOK)
    q = matmul(n1_out[own, :], wq[...], (1, 0))
    q = turned_rows(q, cos[own, :], sin[own, :], False).astype(bf16)
    q_out[...] = q * jnp.asarray(HEAD_DIM ** (-0.5), bf16)
    lse_out[...] = jnp.zeros_like(lse_out)
    lane = lax.broadcasted_iota(jnp.int32, (TOK, 128), 1)

    def heads(j, carry):
        keys = kv_out[:, pl.ds(pl.multiple_of(j * 128, 128), 128)]
        values = kv_out[:, pl.ds(pl.multiple_of(width + j * 128, 128), 128)]
        for g in (0, 1):
            span = pl.ds(pl.multiple_of(j * 256 + g * 128, 128), 128)
            qs = q_out[:, span]
            key = keys[:, g * HEAD_DIM : (g + 1) * HEAD_DIM]
            value = values[:, g * HEAD_DIM : (g + 1) * HEAD_DIM]
            mixed = []
            for h in (0, 1):
                s = matmul(qs[:, h * HEAD_DIM : (h + 1) * HEAD_DIM], key, (1, 1)) + bias[...]
                top = jnp.max(s, axis=1, keepdims=True)
                p = jnp.exp(s - top)
                total = jnp.sum(p, axis=1, keepdims=True)
                p = (p * (1.0 / total)).astype(bf16)
                mixed.append(matmul(p, value, (1, 0)))
                head = j * 4 + g * 2 + h
                lse_out[...] = jnp.where(lane == head, top + jnp.log(total), lse_out[...])
            ho_out[:, span] = jnp.concatenate(mixed, axis=1).astype(bf16)
        return carry

    lax.fori_loop(0, 4, heads, 0)
    r = tok[z].astype(f32) + matmul(ho_out[...], wo[...], (1, 0))
    r_out[...] = r
    n2 = (r * rms_scale(r) * gains[1:2]).astype(bf16)
    n_out[:, :D] = n2
    logits = matmul(n2, small_out[...], (1, 0))
    hits = lane == routes[:, 0:1]
    for k in range(1, routes.shape[1]):
        hits = hits | (lane == routes[:, k : k + 1])
    lifted = jnp.where(hits, logits, masked_score)
    lifted = jnp.where(hits, jnp.exp(lifted - jnp.max(lifted, axis=1, keepdims=True)), 0.0)
    gate = lifted / jnp.sum(lifted, axis=1, keepdims=True)
    gate_out[...] = gate
    row = lax.broadcasted_iota(jnp.int32, (TOK, TOK), 0)
    col = lax.broadcasted_iota(jnp.int32, (TOK, TOK), 1)
    earlier = jnp.where(col < row, 1.0, 0.0).astype(bf16)
    ranks = matmul(earlier, jnp.where(hits, 1.0, 0.0).astype(bf16), (1, 0))
    high = gate.astype(bf16).astype(f32)
    meta = jnp.where(hits, ranks, jnp.where(lane < EXPERTS, -1.0, 0.0))
    meta = meta + pltpu.roll(high, EXPERTS, 1) + pltpu.roll(gate - high, 2 * EXPERTS, 1)
    n_out[:, D:] = meta.astype(bf16)


def front(length, w_q, w_kv, w_o, tok, routes, cos, sin):
    vmem = pl.BlockSpec(memory_space=pltpu.VMEM)
    square = jax.ShapeDtypeStruct((D, D), bf16)
    rows = jax.ShapeDtypeStruct((TOK, D), bf16)
    lanes = jax.ShapeDtypeStruct((TOK, 128), f32)
    return pl.pallas_call(
        front_kernel,
        out_shape=[
            jax.ShapeDtypeStruct((TOK, D + 128), bf16),
            square,
            rows,
            square,
            lanes,
            rows,
            jax.ShapeDtypeStruct((TOK, D), f32),
            lanes,
            square,
            square,
            square,
            jax.ShapeDtypeStruct((D, 128), bf16),
        ],
        in_specs=[pl.BlockSpec(memory_space=pltpu.SMEM)] + [vmem] * 7,
        out_specs=[vmem] * 12,
        scratch_shapes=[pltpu.VMEM((TOK, 4 * TOK), f32)],
        compiler_params=pltpu.CompilerParams(vmem_limit_bytes=56 * 1024 * 1024),
        cost_estimate=pl.CostEstimate(
            flops=10**10, bytes_accessed=30_000_000, transcendentals=5_000_000
        ),
        name="front",
    )(length, w_q, w_kv, w_o, tok, routes, cos, sin)


def rms_back(values, scale, gain, dnormed):
    scaled = values * scale
    dscaled = dnormed * gain
    dvalues = scale * (dscaled - scaled * jnp.mean(dscaled * scaled, axis=-1, keepdims=True))
    return dvalues, jnp.sum(dnormed * scaled, axis=0, keepdims=True)


def pack_into(out, value):
    def chunk(i, carry):
        rows = pl.ds(pl.multiple_of(i * 128, 128), 128)
        left = value[rows, :512].reshape(16, 8, 512)
        right = value[rows, 512:].reshape(16, 8, 512)
        out[pl.ds(i * 16, 16), :, :512] = jnp.concatenate([left, right], axis=1).astype(bf16)
        return carry

    lax.fori_loop(0, 8, chunk, 0)


def back_kernel(
    length, sums, dout, n_ext, r_ref, gate_ref, ho, q_ref, kv, lse, n1, tok, wq, wkv, wo, small,
    cos, sin, cos_t, sin_t,
    dwq_p, dwkv_p, dwo_p, dn1_out, dr_out,
    bias, square, dkv_t, dq_s, do_s, dkv_s,
):
    z = lax.axis_index("seq")
    own = pl.ds(pl.multiple_of(z * TOK, TOK), TOK)
    gains = gain_rows(small[...])
    lane = lax.broadcasted_iota(jnp.int32, (TOK, 128), 1)
    gate = gate_ref[...]
    fields = sums[:, D:]
    dgate = fields + pltpu.roll(fields, 128 - EXPERTS, 1)
    mean = jnp.sum(gate * dgate, axis=1, keepdims=True)
    dlogits = (gate * (dgate - mean)).astype(bf16)
    dn2 = sums[:, :D] + matmul(dlogits, small[...], (1, 1))
    d_router = matmul(n_ext[:, :D], dlogits, (0, 0))
    r = r_ref[...]
    dr, dg2 = rms_back(r, rms_scale(r), gains[1:2], dn2)
    dr = dr + dout[...].astype(f32)
    dr_out[...] = dr
    d_att = dr.astype(bf16)
    square[...] = matmul(ho[...], d_att, (0, 0))
    pack_into(dwo_p, square)
    do_s[...] = matmul(d_att, wo[...], (1, 1)).astype(bf16)
    fill_bias(bias, length[0], z * TOK)
    width = KV_HEADS * HEAD_DIM
    scale = HEAD_DIM ** (-0.5)

    def heads(j, carry):
        keys = kv[:, pl.ds(pl.multiple_of(j * 128, 128), 128)]
        values = kv[:, pl.ds(pl.multiple_of(width + j * 128, 128), 128)]
        for g in (0, 1):
            span = pl.ds(pl.multiple_of(j * 256 + g * 128, 128), 128)
            qs, dos = q_ref[:, span], do_s[:, span]
            prods = dos.astype(f32) * ho[:, span].astype(f32)
            key = keys[:, g * HEAD_DIM : (g + 1) * HEAD_DIM]
            value = values[:, g * HEAD_DIM : (g + 1) * HEAD_DIM]
            dqs = []
            dk_t, dv_t = 0.0, 0.0
            for h in (0, 1):
                part = slice(h * HEAD_DIM, (h + 1) * HEAD_DIM)
                head = j * 4 + g * 2 + h
                shift_by = jnp.sum(jnp.where(lane == head, lse[...], 0.0), axis=1, keepdims=True)
                mine = (lane >= h * HEAD_DIM) & (lane < (h + 1) * HEAD_DIM)
                delta = jnp.sum(jnp.where(mine, prods, 0.0), axis=1, keepdims=True)
                p = jnp.exp(matmul(qs[:, part], key, (1, 1)) + bias[...] - shift_by)
                dp = matmul(dos[:, part], value, (1, 1))
                ds = (p * (dp - delta)).astype(bf16)
                dqs.append(matmul(ds, key, (1, 0)) * scale)
                dk_t = dk_t + matmul(qs[:, part], ds, (0, 0))
                dv_t = dv_t + matmul(dos[:, part], p.astype(bf16), (0, 0))
            dq_s[:, span] = jnp.concatenate(dqs, axis=1)
            half = HEAD_DIM // 2
            wave = dk_t * sin_t[...]
            dk_t = dk_t * cos_t[...] + jnp.concatenate([wave[half:], -wave[:half]], axis=0)
            at = j * 128 + g * HEAD_DIM
            dkv_t[pl.ds(pl.multiple_of(at, HEAD_DIM), HEAD_DIM), :] = dk_t
            dkv_t[pl.ds(pl.multiple_of(width + at, HEAD_DIM), HEAD_DIM), :] = dv_t
        return carry

    lax.fori_loop(0, 4, heads, 0)

    def flip(i, carry):
        at = pl.ds(pl.multiple_of(i * 128, 128), 128)
        dkv_s[:, at] = jnp.transpose(dkv_t[at, :]).astype(bf16)
        return carry

    lax.fori_loop(0, 8, flip, 0)
    dq = turned_rows(dq_s[...], cos[own, :], sin[own, :], True).astype(bf16)
    square[...] = matmul(n1[own, :], dq, (0, 0))
    pack_into(dwq_p, square)
    square[...] = matmul(n1[...], dkv_s[...], (0, 0))
    pack_into(dwkv_p, square)
    square[...] = matmul(dkv_s[...], wkv[...], (1, 1))
    square[own, :] += matmul(dq, wq[...], (1, 1))
    dg1 = jnp.zeros((1, D), f32)
    for b in range(4):
        rows = slice(b * TOK, (b + 1) * TOK)
        x = tok[b].astype(f32)
        dn1 = square[rows, :]
        dg1 = dg1 + jnp.sum(dn1 * (x * rms_scale(x)), axis=0, keepdims=True)
        dn1_out[b] = dn1.astype(bf16)
    sub = lax.broadcasted_iota(jnp.int32, (8, D), 0)
    dgs = jnp.where(sub == 0, dg1, jnp.where(sub == 1, dg2, 0.0))
    high = dgs.astype(bf16)
    low = (dgs - high.astype(f32)).astype(bf16)
    place_lane = lax.broadcasted_iota(jnp.int32, (8, 128), 1)
    place_sub = lax.broadcasted_iota(jnp.int32, (8, 128), 0)
    spread = (place_lane == EXPERTS + place_sub).astype(f32).astype(bf16)
    d_small = d_router + matmul(high, spread, (0, 0)) + matmul(low, spread, (0, 0))
    d_small = d_small.reshape(128, 8, 128)
    dwo_p[:, :, 512:] = jnp.concatenate([d_small, jnp.zeros_like(d_small)], axis=1).astype(bf16)


def back(*args):
    vmem = pl.BlockSpec(memory_space=pltpu.VMEM)
    return pl.pallas_call(
        back_kernel,
        out_shape=[
            jax.ShapeDtypeStruct((128, 16, 512), bf16),
            jax.ShapeDtypeStruct((128, 16, 512), bf16),
            jax.ShapeDtypeStruct((128, 16, 640), bf16),
            jax.ShapeDtypeStruct((4, TOK, D), bf16),
            jax.ShapeDtypeStruct((TOK, D), f32),
        ],
        in_specs=[pl.BlockSpec(memory_space=pltpu.SMEM)] + [vmem] * 19,
        out_specs=[vmem] * 5,
        scratch_shapes=[
            pltpu.VMEM((TOK, 4 * TOK), f32),
            pltpu.VMEM((D, D), f32),
            pltpu.VMEM((D, D), f32),
            pltpu.VMEM((TOK, D), f32),
            pltpu.VMEM((TOK, D), bf16),
            pltpu.VMEM((D, D), bf16),
        ],
        compiler_params=pltpu.CompilerParams(vmem_limit_bytes=60 * 1024 * 1024),
        cost_estimate=pl.CostEstimate(
            flops=2 * 10**10, bytes_accessed=40_000_000, transcendentals=5_000_000
        ),
        name="back",
    )(*args)


def pack_matrix(shard):
    half = shard.shape[1] // 2
    return jnp.concatenate([shard[:, :half], shard[:, half:]], axis=0)


def unpack_matrix(packed):
    return jnp.concatenate([packed[:8], packed[8:]], axis=1)


def body(
    tokens, routes, lengths, out_grad,
    query_weight, query_mean, query_square,
    keyval_weight, keyval_mean, keyval_square,
    output_weight, output_mean, output_square,
    router_weight, router_mean, router_square,
    norm_gains, gains_mean, gains_square,
    gateup_weight, gateup_mean, gateup_square,
    down_weight, down_mean, down_square,
):
    row_count = tokens.shape[0]
    seq_len = row_count * 4
    query_width = HEADS * HEAD_DIM

    small = jnp.concatenate(
        [router_weight, norm_gains.T, jnp.zeros((8, 128 - EXPERTS - 2), f32)], axis=1
    )
    small = jnp.concatenate([small, jnp.zeros((8, 128), f32)], axis=0)
    w_q, w_kv, w_o, all_tokens = gather_front(
        pack_matrix(query_weight).astype(bf16),
        pack_matrix(keyval_weight).astype(bf16),
        jnp.concatenate([pack_matrix(output_weight), small], axis=1).astype(bf16),
        tokens,
    )
    expert_b = lax.all_gather(
        jnp.concatenate([gateup_weight[0], down_weight[0]], axis=0).astype(bf16), "seq", axis=0
    )
    dout_all = lax.all_gather(out_grad, "dp", axis=0)

    cos, sin = rotary_tables(jnp.arange(seq_len, dtype=jnp.int32), HEAD_DIM // 2)
    cos2, sin2 = jnp.tile(cos, (1, 2)), jnp.tile(sin, (1, 2))
    n_ext, n1, q, kv, lse, ho, residual, gate, query_b, keyval_b, output_b, small_b = front(
        lengths,
        w_q.reshape(128, 16, 512),
        w_kv.reshape(128, 16, 512),
        w_o.reshape(128, 16, 640),
        all_tokens,
        routes,
        cos2,
        sin2,
    )
    n_all = gather_plane(n_ext, 2)
    wide = n_all.shape[-1]
    dn_parts, out_parts, d_expert = experts(
        n_all.reshape(EXPERTS, row_count, wide), dout_all, expert_b
    )
    grad_expert = lax.psum_scatter(d_expert, "seq", scatter_dimension=0, tiled=False).astype(f32)
    sums = sum_plane(dn_parts.reshape(4, 4, 2, row_count, wide), 3, f32)
    mixed_out = sum_plane(out_parts.reshape(4, 4, 2, row_count, D), 5, f32)
    layer_out = (residual + mixed_out).astype(bf16)
    d_query, d_keyval, d_last, dn1, dresidual = back(
        lengths, sums, out_grad, n_ext, residual, gate, ho, q, kv, lse, n1, all_tokens,
        query_b, keyval_b, output_b, small_b, cos2, sin2, cos.T, sin.T,
    )
    g_query, g_keyval, g_last, dn1_sum = sum_back(
        (
            d_query.reshape(4, 4, 2, 4, 16, 512),
            d_keyval.reshape(4, 4, 2, 4, 16, 512),
            d_last.reshape(4, 4, 2, 4, 16, 640),
        ),
        dn1,
    )
    grad_query, grad_keyval, grad_output = (
        unpack_matrix(g) for g in (g_query, g_keyval, g_last[:, :512])
    )
    grad_router = g_last[:8, 512 : 512 + EXPERTS]
    grad_gains = g_last[:8, 512 + EXPERTS : 512 + EXPERTS + 2].T
    inputs = tokens.astype(f32)
    gain_one = small_b[:, EXPERTS].astype(f32)
    dnorm_one, _ = norm_back(inputs, rms_scale(inputs), gain_one, dn1_sum)
    tokens_grad = dresidual + dnorm_one

    rate = 0.5
    query_new = adamw(query_weight, grad_query, query_mean, query_square, rate * D ** (-0.5), 0.1)
    keyval_new = adamw(
        keyval_weight, grad_keyval, keyval_mean, keyval_square, rate * D ** (-0.5), 0.1
    )
    output_new = adamw(
        output_weight,
        grad_output,
        output_mean,
        output_square,
        rate * max(1, 2 * query_width // seq_len) ** (-0.5),
        0.1,
    )
    router_new = adamw(
        router_weight, grad_router, router_mean, router_square, rate * (4 * D) ** (-0.5), 0.1
    )
    gains_new = adamw(norm_gains, grad_gains, gains_mean, gains_square, 0.6, 0.0)
    gateup_new = adamw(
        gateup_weight,
        grad_expert[None, : D // 4],
        gateup_mean,
        gateup_square,
        rate * D ** (-0.5),
        0.1,
    )
    down_new = adamw(
        down_weight,
        grad_expert[None, D // 4 :],
        down_mean,
        down_square,
        rate * (FF_E // 8) ** (-0.5),
        0.1,
    )
    return (
        (layer_out, tokens_grad)
        + query_new
        + keyval_new
        + output_new
        + router_new
        + gains_new
        + gateup_new
        + down_new
    )


def solution(mesh):
    rows = P(("dp", "seq"), None)
    gains = P(None, ("dp", "seq"))
    shard = P("dp", "seq", None)
    return jax.shard_map(
        body,
        mesh=mesh,
        in_specs=(rows, rows, P("dp"), rows) + (rows,) * 12 + (gains,) * 3 + (shard,) * 6,
        out_specs=(rows, rows) + (rows,) * 12 + (gains,) * 3 + (shard,) * 6,
        check_vma=False,
    )
```

time: 3260 us -> 484 us (0.15)
  waiting for transfers between devices: 2330 us -> 0.77 us
  Pallas kernels: 0 us -> 444 us
  blocking collectives: 314 us -> 0 us
  local copies, waits for them, and re-layouts: 275 us -> 6.35 us
  other arithmetic: 160 us -> 17.5 us
  matrix products: 129 us -> 0 us
    reduce_scatter x7 -> x1, waiting for transfers between devices: 1910 us -> 0.01 us  [body(): lax.psum_scatter(d_expert, 'seq', scatter_dimension=0, tiled=False)]
    pallas_call x0 -> x8, Pallas kernels: none -> 444 us  [the longest x2 117 us: sum_plane(): pl.pallas_call(sum_plane_kernel, out_shape=jax.ShapeDtypeStruct((rows, wi...]
    all_gather x2 -> x0, blocking collectives: 170 us -> none  [the longest x1 122 us: body(): lax.all_gather(router_weight.astype(bfloat), ('dp', 'seq'), axis=0, tiled...]
    all_gather x6 -> x2, waiting for transfers between devices: 155 us -> 0.04 us  [the longest x1 0.02 us: body(): lax.all_gather(jnp.concatenate([gateup_weight[0], down_weight[0]], axis=0...]
    unnamed x15 -> x3, waiting for transfers between devices: 146 us -> 0.73 us
    dot_general x25 -> x0, matrix products: 129 us -> none  [the longest x1 16.3 us: body(): jnp.einsum('qkgd,pkd->kgqp', dmixed_grouped, values_back, preferred_eleme...]
    all_to_all x3 -> x0, waiting for transfers between devices: 119 us -> none  [the longest x1 73.2 us: body(): lax.all_to_all(drows, 'dp', split_axis=1, concat_axis=0, tiled=True)]
    unnamed x152 -> x69, local copies, waits for them, and re-layouts: 95.8 us -> 4.07 us
  transfers between devices with their start and end apart: 17 -> 3, of which waited for: 14 -> 0; matrix products, arithmetic and copies ran while one was open for 5% -> 3% of each run, Pallas kernels for 0% -> 79%
where the time goes in v1:
time: 484 us; the launch traced here: 483 us
  Pallas kernels  444 us (92%)
  other arithmetic  17.5 us (4%)
  between operations  14.9 us (3%)
  local copies, waits for them, and re-layouts  6.35 us (1%)
    pallas_call x2, Pallas kernels, sum_plane(): pl.pallas_call(sum_plane_kernel, out_shape=jax.ShapeDtypeStruct((rows, wi...  117 us
    pallas_call x1, Pallas kernels, gather_plane(): pl.pallas_call(gather_plane_kernel, out_shape=pltpu.HBM((4, 4, 2) + n.sha...  92.9 us
    pallas_call x1, Pallas kernels, gather_front(): pl.pallas_call(gather_front_kernel, out_shape=shapes, in_specs=[pl.BlockS...  68.6 us
    pallas_call x1, Pallas kernels, experts(): pl.pallas_call(expert_kernel, grid=(sources // GROUP,), out_shape=[jax.Sh...  62.8 us
    pallas_call x1, Pallas kernels, sum_back(): pl.pallas_call(sum_back_kernel, out_shape=[jax.ShapeDtypeStruct((16, w),...  46.7 us
    pallas_call x1, Pallas kernels, back(): pl.pallas_call(back_kernel, out_shape=[jax.ShapeDtypeStruct((128, 16, 512...  32.1 us
    pallas_call x1, Pallas kernels, front(): pl.pallas_call(front_kernel, out_shape=[jax.ShapeDtypeStruct((TOK, D + 12...  23.9 us
  transfers between devices with their start and end apart: 3, of which 0 were waited for; matrix products, arithmetic and copies ran while one was open for 3% of the time, Pallas kernels for 79%

profile of v1, /device:TPU:0, one launch (start us, length us, event | category | flops | bytes accessed | tf_op | source)
XLA Modules:
  0.0 483.2 jit_solution(8457575505085707822)
XLA Ops:
  7.2 1.3 convert.43
  8.6 1.1 convert.44
  9.7 0.9 pad_maximum_fusion
  10.7 0.7 all-gather.6.cloned.1.call-update
  11.7 0.5 multiply_sine_fusion
  12.2 0.9 fusion.16
  13.2 1.0 copy.87.cos
  14.2 1.0 copy.88.sin
  15.9 0.8 copy.86.routes
  16.9 0.6 fusion.15.wo
  17.5 0.6 pad_maximum_fusion.6
  18.1 68.6 %gather_front.1 = (bf16[4,4,2,4,16,512]{5,4,3,2,1,0:T(8,128)(2,1)}, bf16[4,4,2,4,16,512]{5,4,3,2,1,0:T(8,128)(2,1)}, bf16[4,4,2,4,16,640]{5,4,3,2,1,0:T(8,128)(2,1)}, bf16[4,256,1024]{2,1,0:T(8,128)(2,1)}) custom-call(bf16[16,512]{1,0:T(8,128)(2,1)} %get-tuple-element.210.wq, bf16[16,512]{1,0:T(8,128)(2,1)} %get-tuple-element.211.wkv, ...), custom_call_target="tpu_custom_call" | custom-call | tf_op jit(solution)/shard_map/gather_front/pallas_call | solution.py:135
  86.7 23.9 %front.1 = (bf16[256,1152]{1,0:T(8,128)(2,1)}, bf16[1024,1024]{1,0:T(8,128)(2,1)}, bf16[256,1024]{1,0:T(8,128)(2,1)}, bf16[1024,1024]{1,0:T(8,128)(2,1)}, f32[25...) custom-call(s32[1]{0:T(128)S(6)} %copy.98.length, ...), custom_call_target="tpu_custom_call" | custom-call | flops 10000000000 | bytes 30000000 | tf_op jit(solution)/shard_map/front/pallas_call | solution.py:816
  110.6 92.9 %gather_plane.1 = bf16[4,4,2,256,1152]{4,3,2,1,0:T(8,128)(2,1)} custom-call(bf16[256,1152]{1,0:T(8,128)(2,1)} %get-tuple-element.56.n.n_ext), custom_call_target="tpu_custom_call" | custom-call | tf_op jit(solution)/shard_map/gather_plane/pallas_call | solution.py:210
  203.5 62.8 %experts.1 = (bf16[32,256,1152]{2,1,0:T(8,128)(2,1)}, bf16[32,256,1024]{2,1,0:T(8,128)(2,1)}, bf16[4,384,1024]{2,1,0:T(8,128)(2,1)}) custom-call(bf16[32,256,1152]{2,1,0:T(8,128)(2,1)} %bitcast.57, bf16[32,256,1024]{2,1,0:T(8,128)(2,1)} %bitcast.65, bf16[4,384,1024]{2,1,0:T(8,128)(2,1)} %all-gather.4.cloned.1.call-done.w_ref), custom_call_target="tpu_custom_call" | custom-call | flops 28991029248 | bytes 75000000 | tf_op jit(solution)/shard_map/experts/pallas_call | solution.py:658
  267.8 61.7 %sum_plane.3.sums = f32[256,1152]{1,0:T(8,128)} custom-call(bf16[4,4,2,256,1152]{4,3,2,1,0:T(8,128)(2,1)} %bitcast.56), custom_call_target="tpu_custom_call" | custom-call | tf_op jit(solution)/shard_map/sum_plane/pallas_call | solution.py:330
  329.5 32.1 %back.1 = (bf16[128,16,512]{2,1,0:T(8,128)(2,1)}, bf16[128,16,512]{2,1,0:T(8,128)(2,1)}, bf16[128,16,640]{2,1,0:T(8,128)(2,1)}, bf16[4,256,1024]{2,1,0:T(8,128)(2,1)}, f32[256,1024]{1,0:T(8,128)}) custom-call(s32[1]{0:T(128)S(6)} %copy.98.length, f32[256,1152]{1,0:T(8,128)} %sum_plane.3.sums, bf16[256,1024]{1,0:T(8,128)(2,1)} %dout.1, ...), custom_call_target="tpu_custom_call" | custom-call | flops 20000000000 | bytes 40000000 | tf_op jit(solution)/shard_map/back/pallas_call | solution.py:958
  361.6 46.7 %sum_back.1 = (f32[16,512]{1,0:T(8,128)}, f32[16,512]{1,0:T(8,128)}, f32[16,640]{1,0:T(8,128)}, f32[256,1024]{1,0:T(8,128)}) custom-call(bf16[4,4,2,4,16,512]{5,4,3,2,1,0:T(8,128)(2,1)} %bitcast.60, bf16[4,4,2,4,16,512]{5,4,3,2,1,0:T(8,128)(2,1)} %bitcast.61, bf16[4,4,2,4,16,640]{5,4,3,2,1,0:T(8,128)(2,1)} %bitcast.59, ...), custom_call_target="tpu_custom_call" | custom-call | tf_op jit(solution)/shard_map/sum_back/pallas_call | solution.py:482
  408.3 0.8 multiply_subtract_fusion.5
  409.1 0.6 copy.95
  409.7 0.6 copy.96
  410.4 0.6 copy.97
  411.1 54.9 %sum_plane.2 = f32[256,1024]{1,0:T(8,128)} custom-call(bf16[4,4,2,256,1024]{4,3,2,1,0:T(8,128)(2,1)} %bitcast.58), custom_call_target="tpu_custom_call" | custom-call | tf_op jit(solution)/shard_map/sum_plane/pallas_call | solution.py:330
  466.4 0.6 multiply_subtract_fusion.6
  467.1 0.7 multiply_subtract_fusion.2
  467.7 0.7 multiply_subtract_fusion.3
  468.4 0.7 multiply_subtract_fusion.4
  469.0 0.9 add_convert_fusion
  470.0 1.3 fusion.5
  471.2 1.4 convert_element_type.49
  473.0 2.2 multiply_subtract_fusion
  475.2 1.4 multiply_subtract_fusion.1
  (97 shorter events, 2.7 us)
Async XLA Ops:
  7.2 196.3 %all-gather.4.cloned.1.call-start = ((), (), s32[]{:S(2)}) async-start(), calls=%async_computation.1 | async-start | bytes 3932160 | tf_op jit(solution)/shard_map/all_gather | solution.py:1018
  8.5 2.9 copy-start.13
  8.6 2.9 copy-start.14
  8.6 2.9 copy-start.12
  8.6 2.9 copy-start.28
  8.6 3.1 copy-start.24
  10.7 192.9 %all-gather.6.cloned.1.call-start = ((), (), s32[]{:S(2)}) async-start(), calls=%async_computation.3 | async-start | bytes 17301504 | tf_op jit(solution)/shard_map/all_gather | solution.py:1021
  11.4 459.8 %reduce-scatter.2.cloned.1.call-start = ((), (), s32[]{:S(2)}) async-start(), calls=%async_computation.2 | async-start | bytes 3932160 | tf_op jit(solution)/shard_map/reduce_scatter | solution.py:1040
  13.1 2.8 copy-start.25
  266.4 1.0 copy-start.11
  266.4 1.2 copy-start
  411.0 55.0 %copy-start.3 = (f32[256,1024]{1,0:T(8,128)S(1)}, f32[256,1024]{1,0:T(8,128)}, u32[]{:S(2)}) copy-start(f32[256,1024]{1,0:T(8,128)} %get-tuple-element.74) | copy-start | bytes 3145732
  411.0 55.3 %copy-start.15 = (f32[16,640]{1,0:T(8,128)S(1)}, f32[16,640]{1,0:T(8,128)}, u32[]{:S(2)}) copy-start(f32[16,640]{1,0:T(8,128)} %get-tuple-element.77) | copy-start | bytes 122884
  411.0 55.4 %copy-start.26 = (f32[8,32]{1,0:T(8,128)S(1)}, f32[8,32]{1,0:T(8,128)}, u32[]{:S(2)}) copy-start(f32[8,32]{1,0:T(8,128)} %param.39) | copy-start | bytes 3076
  411.0 55.4 %copy-start.27 = (f32[8,32]{1,0:T(8,128)S(1)}, f32[8,32]{1,0:T(8,128)}, u32[]{:S(2)}) copy-start(f32[8,32]{1,0:T(8,128)} %param.40) | copy-start | bytes 3076
  411.0 56.0 %copy-start.23 = (f32[16,512]{1,0:T(8,128)S(1)}, f32[16,512]{1,0:T(8,128)}, u32[]{:S(2)}) copy-start(f32[16,512]{1,0:T(8,128)} %get-tuple-element.76) | copy-start | bytes 98308
  411.0 56.0 %copy-start.22 = (f32[16,512]{1,0:T(8,128)S(1)}, f32[16,512]{1,0:T(8,128)}, u32[]{:S(2)}) copy-start(f32[16,512]{1,0:T(8,128)} %get-tuple-element.75) | copy-start | bytes 98308
  411.0 56.0 %copy-start.16 = (f32[8,1024]{1,0:T(8,128)S(1)}, f32[8,1024]{1,0:T(8,128)}, u32[]{:S(2)}) copy-start(f32[8,1024]{1,0:T(8,128)} %param.36) | copy-start | bytes 98308
  411.1 56.0 %copy-start.17 = (f32[8,1024]{1,0:T(8,128)S(1)}, f32[8,1024]{1,0:T(8,128)}, u32[]{:S(2)}) copy-start(f32[8,1024]{1,0:T(8,128)} %param.37) | copy-start | bytes 98308
  411.1 56.7 %copy-start.18 = (f32[8,1024]{1,0:T(8,128)S(1)}, f32[8,1024]{1,0:T(8,128)}, u32[]{:S(2)}) copy-start(f32[8,1024]{1,0:T(8,128)} %param.33) | copy-start | bytes 98308
  411.1 56.6 %copy-start.19 = (f32[8,1024]{1,0:T(8,128)S(1)}, f32[8,1024]{1,0:T(8,128)}, u32[]{:S(2)}) copy-start(f32[8,1024]{1,0:T(8,128)} %param.34) | copy-start | bytes 98308
  466.0 2.4 copy-start.20
  466.0 2.4 copy-start.21
  466.0 3.0 copy-start.2
  466.0 3.0 copy-start.7
  466.3 3.6 copy-start.8
  470.0 2.7 copy-start.6
  471.2 1.5 copy-start.1
  471.2 1.8 copy-start.5
  473.0 2.2 copy-start.4
  473.0 2.2 copy-start.9
  473.0 2.2 copy-start.10
  (2 other events, 1.4 us)
Sparse Core Ops, SparseCore 0:
  10.8 74.2 all-gather.3
  87.4 110.3 all-gather.5
  266.6 35.1 reduce-scatter.1

commit v2 on v1

--- a/solution.py
+++ b/solution.py
@@ -9,15 +9,15 @@
 bf16 = jnp.bfloat16
 f32 = jnp.float32
 AXES = "xycz"
+STRIP = 16
 
 
 def place():
-    dp = lax.axis_index("dp")
-    return {"x": dp // 8, "y": (dp // 2) % 4, "c": dp % 2, "z": lax.axis_index("seq")}
+    return {a: lax.axis_index(a) for a in AXES}
 
 
 def device(at):
-    return ((at["x"] * 4 + at["y"]) * 2 + at["c"], at["z"])
+    return tuple(at[a] for a in AXES)
 
 
 def shift(at, axis, by):
@@ -42,7 +42,7 @@
 
 
 class Wires:
-    def __init__(self, send_sems, recv_sems, local_sems=None):
+    def __init__(self, send_sems, recv_sems, local_sems):
         self.send_sems, self.recv_sems, self.local_sems = send_sems, recv_sems, local_sems
         self.copies, self.local = [], 0
 
@@ -71,160 +71,190 @@
             copy.wait_send()
 
 
+def wire_sems(copies, kept):
+    return [
+        pltpu.SemaphoreType.DMA((copies,)),
+        pltpu.SemaphoreType.DMA((copies,)),
+        pltpu.SemaphoreType.DMA((kept,)),
+    ]
+
+
+def in_order(order, **steps):
+    for letter in order:
+        next(steps[letter], None)
+    for step in steps.values():
+        for _ in step:
+            pass
+
+
+def hbm(*arrays):
+    return [pltpu.with_memory_space_constraint(v, pltpu.HBM) for v in arrays]
+
+
+def ring_steps(wires, at, axis, spot, hand_on):
+    right, left = peer(at, axis, 1), peer(at, axis, 3)
+    to_right = {k: wires.send(spot(0, k), spot(0, k), right) for k in (0, 1)}
+    to_left = {k: wires.send(spot(0, k), spot(0, k), left) for k in (1, 0)}
+    for k in (0, 1):
+        hand_on(0, k)
+    yield
+    to_right[0].wait_recv()
+    far_right = wires.send(spot(3, 0), spot(3, 0), right)
+    hand_on(3, 0)
+    to_left[1].wait_recv()
+    far_left = wires.send(spot(1, 1), spot(1, 1), left)
+    hand_on(1, 1)
+    yield
+    to_right[1].wait_recv()
+    hand_on(3, 1)
+    to_left[0].wait_recv()
+    hand_on(1, 0)
+    yield
+    far_right.wait_recv()
+    hand_on(2, 0)
+    far_left.wait_recv()
+    hand_on(2, 1)
+
+
+def row_steps(wires, at, src, out):
+    half = src.shape[0] // 2
+    own = out.at[at["x"], at["c"]]
+    kept = wires.keep(src, own)
+    sibling = peer(at, "c", 1)
+    across = []
+
+    def spot(by, part):
+        return out.at[shift(at, "x", by), at["c"], pl.ds(part * half, half)]
+
+    def hand_on(by, part):
+        across.append(wires.send(spot(by, part), spot(by, part), sibling))
+
+    kept.wait()
+    yield from ring_steps(wires, at, "x", spot, hand_on)
+    yield
+    for copy in across:
+        copy.wait_recv()
+
+
+ROW_COPIES = 6 + 8
+
+
+def token_steps(wires, at, src, out):
+    half = src.shape[0] // 2
+    kept = wires.keep(src, out.at[at["z"]])
+
+    def spot(by, part):
+        return out.at[shift(at, "z", by), pl.ds(part * half, half)]
+
+    kept.wait()
+    yield from ring_steps(wires, at, "z", spot, lambda by, part: None)
+
+
+TOKEN_COPIES = 6
+
+
 def index(at, whole, **fixed):
-    spots = {**at, **fixed}
-    return tuple(slice(None) if axis in whole else spots[axis] for axis in AXES)
-
-
-GATHER_ORDERS = ("zyx", "xzy", "yxz")
-
-
-def gather_front_kernel(
-    wq, wkv, wo, tok, oq, okv, oo, ot, send_sems, recv_sems, local_sems
-):
-    at = place()
-    wires = Wires(send_sems, recv_sems, local_sems)
-    parts = list(zip((wq, wkv, wo), (oq, okv, oo), GATHER_ORDERS))
+    spots = {**at, **{a: slice(None) for a in whole}, **fixed}
+    return tuple(spots[axis] for axis in AXES)
+
+
+def weight_steps(wires, at, parts):
     kept = [wires.keep(w, o.at[index(at, "")]) for w, o, _ in parts]
-    kept.append(wires.keep(tok, ot.at[at["z"]]))
-    greet(at, "xyzc")
     arrivals = {}
     for p, (w, o, order) in enumerate(parts):
         for by in (1, 3, 2):
             arrivals[p, by] = wires.send(w, o.at[index(at, "")], peer(at, order[0], by))
-    half = tok.shape[0] // 2
-    low, high = pl.ds(0, half), pl.ds(half, half)
-    z = at["z"]
-    from_left = wires.send(tok, ot.at[z], peer(at, "z", 1))
-    from_right = wires.send(tok, ot.at[z], peer(at, "z", 3))
+    yield
     for copy in kept:
         copy.wait()
-    for stage in (1, 2):
-        later = {}
-        for p, (w, o, order) in enumerate(parts):
-            for by in (1, 3, 2):
-                arrivals[p, by].wait_recv()
-            spot = index(at, order[:stage])
-            for by in (1, 3, 2):
-                later[p, by] = wires.send(o.at[spot], o.at[spot], peer(at, order[stage], by))
-        arrivals = later
+    later = {}
+    for p, (w, o, order) in enumerate(parts):
+        for by in (1, 3, 2):
+            arrivals[p, by].wait_recv()
+        spot = index(at, order[0])
+        for by in (1, 3, 2):
+            later[p, by] = wires.send(o.at[spot], o.at[spot], peer(at, order[1], by))
+    yield
     sibling = peer(at, "c", 1)
-    across = []
+    across, rings = [], []
     for p, (w, o, order) in enumerate(parts):
-        spot = index(at, order[:2])
-        across.append(wires.send(o.at[spot], o.at[spot], sibling))
-    from_left.wait_recv()
-    left, right = shift(at, "z", 3), shift(at, "z", 1)
-    far = [wires.send(ot.at[left, low], ot.at[left, low], peer(at, "z", 1))]
-    from_right.wait_recv()
-    far.append(wires.send(ot.at[right, high], ot.at[right, high], peer(at, "z", 3)))
-    for by in (1, 3, 2):
-        for p, (w, o, order) in enumerate(parts):
-            arrivals[p, by].wait_recv()
-            spot = index(at, order[:2], **{order[2]: shift(at, order[2], 4 - by)})
-            across.append(wires.send(o.at[spot], o.at[spot], sibling))
-    for copy in far + across:
+        for by in (1, 3, 2):
+            later[p, by].wait_recv()
+
+        def spot(by, part, o=o, order=order):
+            pieces = {order[1]: pl.ds(2 * part, 2), order[2]: shift(at, order[2], by)}
+            return o.at[index(at, order[0], **pieces)]
+
+        def hand_on(by, part, spot=spot):
+            across.append(wires.send(spot(by, part), spot(by, part), sibling))
+
+        ring = ring_steps(wires, at, order[2], spot, hand_on)
+        next(ring)
+        rings.append(ring)
+    yield
+    for _ in range(3):
+        for ring in rings:
+            next(ring, None)
+        yield
+    for copy in across:
         copy.wait_recv()
+
+
+WEIGHT_COPIES = 3 * (3 + 3 + 6 + 8)
+
+
+GATHER_ORDERS = ("zyx", "zxy", "zyx")
+GATHER_SCHEDULE = "wtdwwdtwdwtd"
+
+
+def gather_front_kernel(wq, wkv, wo, tok, dout, oq, okv, oo, ot, od, *sems):
+    at = place()
+    wires = Wires(*sems)
+    greet(at, "xyzc")
+    in_order(
+        GATHER_SCHEDULE,
+        w=weight_steps(wires, at, list(zip((wq, wkv, wo), (oq, okv, oo), GATHER_ORDERS))),
+        t=token_steps(wires, at, tok, ot),
+        d=row_steps(wires, at, dout, od),
+    )
     wires.finish()
 
 
-def gather_front(wq, wkv, wo, tok):
+def gather_front(wq, wkv, wo, tok, dout):
     shapes = [pltpu.HBM((4, 4, 2, 4) + w.shape, w.dtype) for w in (wq, wkv, wo)]
     shapes.append(pltpu.HBM((4,) + tok.shape, tok.dtype))
-    count = 9 * 3 + 4 + 12
+    shapes.append(pltpu.HBM((4, 2) + dout.shape, dout.dtype))
+    far = pl.BlockSpec(memory_space=pltpu.HBM)
     return pl.pallas_call(
         gather_front_kernel,
         out_shape=shapes,
-        in_specs=[pl.BlockSpec(memory_space=pltpu.HBM)] * 4,
-        out_specs=[pl.BlockSpec(memory_space=pltpu.HBM)] * 4,
-        scratch_shapes=[
-            pltpu.SemaphoreType.DMA((count,)),
-            pltpu.SemaphoreType.DMA((count,)),
-            pltpu.SemaphoreType.DMA((4,)),
-        ],
+        in_specs=[far] * 5,
+        out_specs=[far] * 5,
+        scratch_shapes=wire_sems(WEIGHT_COPIES + TOKEN_COPIES + ROW_COPIES, 5),
         compiler_params=pltpu.CompilerParams(collective_id=1, has_side_effects=True),
         name="gather_front",
-    )(*(pltpu.with_memory_space_constraint(v, pltpu.HBM) for v in (wq, wkv, wo, tok)))
-
-
-PLANE_ORDERS = ("xy", "yx")
-
-
-def gather_plane_kernel(n, o, send_sems, recv_sems, local_sems):
+    )(*hbm(wq, wkv, wo, tok, dout))
+
+
+def gather_rows_kernel(n, o, *sems):
     at = place()
-    wires = Wires(send_sems, recv_sems, local_sems)
-    half = n.shape[0] // 2
-    rows = [pl.ds(0, half), pl.ds(half, half)]
-
-    def spot(h, **fixed):
-        where = {**at, **fixed}
-        return o.at[where["x"], where["y"], where["c"], rows[h]]
-
-    mine = o.at[at["x"], at["y"], at["c"]]
-    kept = wires.keep(n, mine)
-    greet(at, "xyc")
-    sibling = peer(at, "c", 1)
-    first, second, across = {}, {}, []
-    for by in (1, 3, 2):
-        for h in (0, 1):
-            axis = PLANE_ORDERS[h][0]
-            first[h, by] = wires.send(n.at[rows[h]], spot(h), peer(at, axis, by))
-    for h in (0, 1):
-        axis = PLANE_ORDERS[h][1]
-        for to in (1, 3):
-            second[h, 0, to] = wires.send(n.at[rows[h]], spot(h), peer(at, axis, to))
-    across.append(wires.send(n, mine, sibling))
-    for by in (1, 3, 2):
-        for h in (0, 1):
-            one, two = PLANE_ORDERS[h]
-            first[h, by].wait_recv()
-            unit = spot(h, **{one: shift(at, one, 4 - by)})
-            for to in (1, 3):
-                second[h, by, to] = wires.send(unit, unit, peer(at, two, to))
-            across.append(wires.send(unit, unit, sibling))
-    far = []
-    for by in (0, 1, 3, 2):
-        for h in (0, 1):
-            one, two = PLANE_ORDERS[h]
-            for to in (1, 3):
-                second[h, by, to].wait_recv()
-                unit = spot(
-                    h, **{one: shift(at, one, (4 - by) % 4), two: shift(at, two, 4 - to)}
-                )
-                if (to == 1) == (by in (0, 3)):
-                    far.append(((h, by, to), wires.send(unit, unit, peer(at, two, to))))
-                across.append(wires.send(unit, unit, sibling))
-    for (h, by, to), copy in far:
-        one, two = PLANE_ORDERS[h]
-        copy.wait_recv()
-        unit = spot(h, **{one: shift(at, one, (4 - by) % 4), two: shift(at, two, 2)})
-        across.append(wires.send(unit, unit, sibling))
-    for copy in across:
-        copy.wait_recv()
-    kept.wait()
+    wires = Wires(*sems)
+    greet(at, "xc")
+    in_order("", d=row_steps(wires, at, n, o))
     wires.finish()
 
 
-def gather_plane(n, collective_id):
-    count = 6 + 16 + 8 + 31
+def gather_rows(n):
+    far = pl.BlockSpec(memory_space=pltpu.HBM)
     return pl.pallas_call(
-        gather_plane_kernel,
-        out_shape=pltpu.HBM((4, 4, 2) + n.shape, n.dtype),
-        in_specs=[pl.BlockSpec(memory_space=pltpu.HBM)],
-        out_specs=pl.BlockSpec(memory_space=pltpu.HBM),
-        scratch_shapes=[
-            pltpu.SemaphoreType.DMA((count,)),
-            pltpu.SemaphoreType.DMA((count,)),
-            pltpu.SemaphoreType.DMA((1,)),
-        ],
-        compiler_params=pltpu.CompilerParams(
-            collective_id=collective_id, has_side_effects=True
-        ),
-        name="gather_plane",
-    )(pltpu.with_memory_space_constraint(n, pltpu.HBM))
-
-
-STRIP = 16
+        gather_rows_kernel,
+        out_shape=pltpu.HBM((4, 2) + n.shape, n.dtype),
+        in_specs=[far],
+        out_specs=far,
+        scratch_shapes=wire_sems(ROW_COPIES, 1),
+        compiler_params=pltpu.CompilerParams(collective_id=2, has_side_effects=True),
+        name="gather_rows",
+    )(*hbm(n))
 
 
 def add_rows(out, parts, rows):
@@ -239,149 +269,102 @@
     lax.fori_loop(0, rows // STRIP, strip, 0)
 
 
-def sum_plane_kernel(
-    c_ref, out, held, crossed, near, mid, last, send_sems, recv_sems, local_sems
-):
+def ring_sum_steps(wires, at, axis, blocks, out, mid, last, near):
+    half = out.shape[0] // 2
+    low, high = pl.ds(0, half), pl.ds(half, half)
+    ahead, back, far = (blocks.at[shift(at, axis, by)] for by in (1, 3, 2))
+    right, left = peer(at, axis, 1), peer(at, axis, 3)
+    near_l = wires.send(far.at[low], near.at[0], right)
+    near_r = wires.send(far.at[high], near.at[1], left)
+    pure_l = wires.send(ahead.at[high], last.at[0, high], right)
+    pure_r = wires.send(back.at[low], last.at[1, low], left)
+    yield
+    near_l.wait_recv()
+    add_rows(mid.at[0], [ahead.at[low], near.at[0]], half)
+    sum_l = wires.send(mid.at[0], last.at[0, low], right)
+    near_r.wait_recv()
+    add_rows(mid.at[1], [back.at[high], near.at[1]], half)
+    sum_r = wires.send(mid.at[1], last.at[1, high], left)
+    yield
+    for copy in (pure_l, sum_l, pure_r, sum_r):
+        copy.wait_recv()
+    add_rows(out, [blocks.at[at[axis]], last.at[0], last.at[1]], 2 * half)
+
+
+def ring_sum_scratch(rows, width):
+    return [
+        pltpu.VMEM((2, rows // 2, width), bf16),
+        pltpu.VMEM((2, rows, width), bf16),
+        pltpu.VMEM((2, rows // 2, width), bf16),
+    ]
+
+
+def row_sum_steps(wires, at, c_ref, out, held, crossed, mid, last, near):
+    other = shift(at, "c", 1)
+    sibling = peer(at, "c", 1)
+    rows = out.shape[0]
+    crossing, kept = {}, {}
+    for by in (2, 1, 3, 0):
+        i = shift(at, "x", by)
+        crossing[by] = wires.send(c_ref.at[i, other], crossed.at[i], sibling)
+        kept[by] = wires.keep(c_ref.at[i, at["c"]], held.at[i])
+    yield
+    for by in (2, 1, 3, 0):
+        i = shift(at, "x", by)
+        kept[by].wait()
+        crossing[by].wait_recv()
+        add_rows(held.at[i], [held.at[i], crossed.at[i]], rows)
+        if by == 3:
+            ring = ring_sum_steps(wires, at, "x", held, out, mid, last, near)
+            next(ring)
+    yield
+    yield from ring
+
+
+ROW_SUM_COPIES = 4 + 6
+
+
+def row_sum_scratch(rows, width):
+    return [pltpu.VMEM((4, rows, width), bf16)] * 2 + ring_sum_scratch(rows, width)
+
+
+def sum_rows_kernel(c_ref, out, *refs):
     at = place()
-    wires = Wires(send_sems, recv_sems, local_sems)
-    whole = out.shape[0]
-    half = whole // 2
-    rows = [pl.ds(0, half), pl.ds(half, half)]
-    orders = ("yx", "xy")
-    blocks = [(2, 2), (0, 2), (2, 0), (1, 2), (2, 1), (3, 2), (2, 3)]
-    blocks += [(0, 1), (1, 0), (0, 3), (3, 0), (1, 1), (3, 3), (1, 3), (3, 1), (0, 0)]
-    other = shift(at, "c", 1)
-
-    def spot(dx, dy):
-        return shift(at, "x", dx), shift(at, "y", dy)
-
-    kept = [
-        wires.keep(c_ref.at[spot(*b) + (at["c"],)], held.at[spot(*b)]) for b in blocks
-    ]
-    greet(at, "xyc")
-    sibling = peer(at, "c", 1)
-    crossing = {}
-    for b in blocks:
-        crossing[b] = wires.send(
-            c_ref.at[spot(*b) + (other,)], crossed.at[spot(*b)], sibling
-        )
-
-    def unit(h, d1, d2):
-        dx, dy = (d2, d1) if h == 0 else (d1, d2)
-        return held.at[spot(dx, dy) + (rows[h],)]
-
-    step1, step2 = {}, {}
-
-    def settle(b, number):
-        kept[number].wait()
-        crossing[b].wait_recv()
-        add_rows(held.at[spot(*b)], [held.at[spot(*b)], crossed.at[spot(*b)]], whole)
-
-    for number, b in enumerate(blocks):
-        settle(b, number)
-        for h in (0, 1):
-            d1, d2 = (b[1], b[0]) if h == 0 else (b[0], b[1])
-            axis = orders[h][0]
-            if d1 == 2:
-                to = 1 if d2 < 2 else 3
-                step1[h, d2] = wires.send(
-                    unit(h, 2, d2), near.at[h, d2], peer(at, axis, to)
-                )
-            elif (d1 == 1 and d2 >= 2) or (d1 == 3 and d2 < 2):
-                step2[h, d1, d2] = wires.send(
-                    unit(h, d1, d2), mid.at[h, d1 // 2, d2], peer(at, axis, d1)
-                )
-    for d2 in (0, 2, 1, 3):
-        for h in (0, 1):
-            d1 = 1 if d2 < 2 else 3
-            axis = orders[h][0]
-            step1[h, d2].wait_recv()
-            add_rows(unit(h, d1, d2), [unit(h, d1, d2), near.at[h, d2]], half)
-            step2[h, d1, d2] = wires.send(
-                unit(h, d1, d2), mid.at[h, d1 // 2, d2], peer(at, axis, d1)
-            )
-    ends = {}
-    for d2 in (2, 1, 3, 0):
-        for h in (0, 1):
-            for d1 in (1, 3):
-                step2[h, d1, d2].wait_recv()
-            add_rows(
-                unit(h, 0, d2), [unit(h, 0, d2), mid.at[h, 0, d2], mid.at[h, 1, d2]], half
-            )
-            if d2:
-                ends[h, d2] = wires.send(
-                    unit(h, 0, d2), last.at[h, d2 - 1], peer(at, orders[h][1], d2)
-                )
-    for h in (0, 1):
-        for d2 in (1, 3, 2):
-            ends[h, d2].wait_recv()
-        add_rows(
-            out.at[rows[h]],
-            [unit(h, 0, 0), last.at[h, 0], last.at[h, 1], last.at[h, 2]],
-            half,
-        )
+    wires = Wires(*refs[-3:])
+    greet(at, "xc")
+    in_order("", p=row_sum_steps(wires, at, c_ref, out, *refs[:5]))
     wires.finish()
 
 
-def sum_plane(c, collective_id, dtype):
+def sum_rows(c):
     rows, width = c.shape[-2:]
-    half = rows // 2
-    count = 16 + 8 + 16 + 6
     return pl.pallas_call(
-        sum_plane_kernel,
-        out_shape=jax.ShapeDtypeStruct((rows, width), dtype),
+        sum_rows_kernel,
+        out_shape=jax.ShapeDtypeStruct((rows, width), f32),
         in_specs=[pl.BlockSpec(memory_space=pltpu.HBM)],
         out_specs=pl.BlockSpec(memory_space=pltpu.VMEM),
-        scratch_shapes=[
-            pltpu.VMEM((4, 4, rows, width), bf16),
-            pltpu.VMEM((4, 4, rows, width), bf16),
-            pltpu.VMEM((2, 4, half, width), bf16),
-            pltpu.VMEM((2, 2, 4, half, width), bf16),
-            pltpu.VMEM((2, 3, half, width), bf16),
-            pltpu.SemaphoreType.DMA((count,)),
-            pltpu.SemaphoreType.DMA((count,)),
-            pltpu.SemaphoreType.DMA((16,)),
-        ],
+        scratch_shapes=row_sum_scratch(rows, width) + wire_sems(ROW_SUM_COPIES, 4),
         compiler_params=pltpu.CompilerParams(
-            collective_id=collective_id,
-            has_side_effects=True,
-            vmem_limit_bytes=56 * 1024 * 1024,
+            collective_id=3, has_side_effects=True, vmem_limit_bytes=56 * 1024 * 1024
         ),
-        name="sum_plane",
-    )(pltpu.with_memory_space_constraint(c, pltpu.HBM))
-
-
-SUM_ORDERS = ("xyz", "yzx", "zxy")
+        name="sum_rows",
+    )(*hbm(c))
+
+
+SUM_ORDERS = ("yxz", "xyz", "zxy")
+SUM_SCHEDULE = "mnpmmmpnpmmmmmm"
 
 
 def pick(ref, axes, axis, mine):
     return ref.at[tuple(mine if a == axis else slice(None) for a in axes)]
 
 
-def sum_back_kernel(*refs):
-    mats, dn1 = refs[0:3], refs[3]
-    outs, dn1_out = refs[4:7], refs[7]
-    scratch = refs[8:-3]
-    send_sems, recv_sems, local_sems = refs[-3:]
-    crossed, held, one, two, three, sum1, sum2 = [scratch[i * 3 : i * 3 + 3] for i in range(7)]
-    zmid, zlast, znear = scratch[21:24]
-    at = place()
-    wires = Wires(send_sems, recv_sems, local_sems)
-    greet(at, "xyzc")
+def mat_steps(wires, at, mats, outs, crossed, held, one, two, three, sum1, sum2):
     sibling = peer(at, "c", 1)
     other = shift(at, "c", 1)
     crossing = [
         wires.send(mats[p].at[:, :, other], crossed[p], sibling) for p in range(3)
     ]
-    half = dn1.shape[1] // 2
-    low, high = pl.ds(0, half), pl.ds(half, half)
-    z = at["z"]
-    ahead, back, far = shift(at, "z", 1), shift(at, "z", 3), shift(at, "z", 2)
-    up, down = peer(at, "z", 1), peer(at, "z", 3)
-    znear_l = wires.send(dn1.at[far, low], znear.at[0], up)
-    znear_r = wires.send(dn1.at[far, high], znear.at[1], down)
-    zpure_l = wires.send(dn1.at[ahead, high], zlast.at[0, high], up)
-    zpure_r = wires.send(dn1.at[back, low], zlast.at[1, low], down)
 
     def total(out, parts, count):
         def body(i, carry):
@@ -394,6 +377,7 @@
         lax.fori_loop(0, count, body, 0)
 
     stage1 = {}
+    yield
     for p in range(3):
         crossing[p].wait_recv()
 
@@ -412,12 +396,7 @@
                 one[p].at[by - 1],
                 peer(at, axis, by),
             )
-    znear_l.wait_recv()
-    add_rows(zmid.at[0], [dn1.at[ahead, low], znear.at[0]], half)
-    zsum_l = wires.send(zmid.at[0], zlast.at[0, low], up)
-    znear_r.wait_recv()
-    add_rows(zmid.at[1], [dn1.at[back, high], znear.at[1]], half)
-    zsum_r = wires.send(zmid.at[1], zlast.at[1, high], down)
+        yield
     stage2 = {}
     for p in range(3):
         axis, after = SUM_ORDERS[p][0], SUM_ORDERS[p][1]
@@ -435,6 +414,7 @@
                 two[p].at[by - 1],
                 peer(at, after, by),
             )
+        yield
     stage3 = {}
     for p in range(3):
         axis, after, end = SUM_ORDERS[p]
@@ -450,9 +430,7 @@
             stage3[p, by] = wires.send(
                 sum2[p].at[shift(at, end, by)], three[p].at[by - 1], peer(at, end, by)
             )
-    for copy in (zpure_l, zsum_l, zpure_r, zsum_r):
-        copy.wait_recv()
-    add_rows(dn1_out, [dn1.at[z], zlast.at[0], zlast.at[1]], 2 * half)
+        yield
     for p in range(3):
         for by in (1, 3, 2):
             stage3[p, by].wait_recv()
@@ -460,37 +438,45 @@
         for k in range(3):
             value = value + three[p][k].astype(f32)
         outs[p][...] = value
+
+
+def sum_back_kernel(*refs):
+    mats, dn1, c_ref = refs[0:3], refs[3], refs[4]
+    outs, dn1_out, mixed_out = refs[5:8], refs[8], refs[9]
+    scratch = refs[10:-3]
+    groups = [scratch[i * 3 : i * 3 + 3] for i in range(7)]
+    at = place()
+    wires = Wires(*refs[-3:])
+    greet(at, "xyzc")
+    in_order(
+        SUM_SCHEDULE,
+        p=row_sum_steps(wires, at, c_ref, mixed_out, *scratch[24:29]),
+        m=mat_steps(wires, at, mats, outs, *groups),
+        n=ring_sum_steps(wires, at, "z", dn1, dn1_out, *scratch[21:24]),
+    )
     wires.finish()
 
 
-def sum_back(mats, dn1):
+def sum_back(mats, dn1, c):
     widths = [m.shape[-1] for m in mats]
     rows, model = dn1.shape[1:]
-    count = 3 * 10 + 6
     scratch = []
     for lead in ((4, 4, 4), (4, 4, 4), (3, 4, 4), (3, 4), (3,), (4, 4), (4,)):
         scratch += [pltpu.VMEM(lead + (16, w), bf16) for w in widths]
-    scratch += [
-        pltpu.VMEM((2, rows // 2, model), bf16),
-        pltpu.VMEM((2, rows, model), bf16),
-        pltpu.VMEM((2, rows // 2, model), bf16),
-        pltpu.SemaphoreType.DMA((count,)),
-        pltpu.SemaphoreType.DMA((count,)),
-        pltpu.SemaphoreType.DMA((1,)),
-    ]
+    scratch += ring_sum_scratch(rows, model) + row_sum_scratch(rows, model)
     vmem = pl.BlockSpec(memory_space=pltpu.VMEM)
     return pl.pallas_call(
         sum_back_kernel,
         out_shape=[jax.ShapeDtypeStruct((16, w), f32) for w in widths]
-        + [jax.ShapeDtypeStruct((rows, model), f32)],
-        in_specs=[vmem] * 4,
-        out_specs=[vmem] * 4,
-        scratch_shapes=scratch,
+        + [jax.ShapeDtypeStruct((rows, model), f32)] * 2,
+        in_specs=[vmem] * 4 + [pl.BlockSpec(memory_space=pltpu.HBM)],
+        out_specs=[vmem] * 5,
+        scratch_shapes=scratch + wire_sems(3 * 10 + 6 + ROW_SUM_COPIES, 4),
         compiler_params=pltpu.CompilerParams(
-            collective_id=4, has_side_effects=True, vmem_limit_bytes=56 * 1024 * 1024
+            collective_id=4, has_side_effects=True, vmem_limit_bytes=60 * 1024 * 1024
         ),
         name="sum_back",
-    )(*mats, dn1)
+    )(*mats, dn1, *hbm(c))
 
 
 D = 1024
@@ -571,7 +557,10 @@
     return (weight - rate * (update + decay * weight), first_new, second_new)
 
 
-GROUP = 4
+SOURCES = 8
+HOSTED = 4
+SLOTS = SOURCES * CAP
+OUT_BLOCKS = 2
 
 
 def matmul(a, b, contract):
@@ -580,104 +569,128 @@
     )
 
 
-def expert_kernel(n_ref, g_ref, w_ref, dn_ref, out_ref, dw_ref, xs, ds, dzs, gys, acc_gu, acc_d):
+def expert_kernel(n_ref, g_ref, w_ref, dn_ref, out_ref, dw_ref, xs, ds, zs, gates):
     step = pl.program_id(0)
-    expert = lax.axis_index("dp")
+    base = lax.axis_index("x") * 8 + lax.axis_index("c")
 
     @pl.when(step == 0)
     def _():
-        acc_gu[...] = jnp.zeros_like(acc_gu)
-        acc_d[...] = jnp.zeros_like(acc_d)
-
-    lane8 = lax.broadcasted_iota(jnp.int32, (8, 128), 1)
-    sub8 = lax.broadcasted_iota(jnp.int32, (8, 128), 0)
-    choose = (lane8 == expert + EXPERTS * sub8).astype(f32).astype(bf16)
-    slot_row = lax.broadcasted_iota(jnp.int32, (CAP, TOK), 0).astype(f32)
-    gates = []
-    for b in range(GROUP):
-        meta = n_ref[b, :, D:]
-        fields = matmul(choose, meta, (1, 1))
-        hot = slot_row == fields[0:1]
-        pick_rows = jnp.where(hot, 1.0, 0.0).astype(bf16)
-        gate_row = fields[1:2] + fields[2:3]
-        gates.append(jnp.sum(jnp.where(hot, gate_row, 0.0), axis=1, keepdims=True))
-        span = pl.ds(b * CAP, CAP)
-        xs[span, :] = matmul(pick_rows, n_ref[b, :, :D], (1, 0)).astype(bf16)
-        ds[span, :] = matmul(pick_rows, g_ref[b], (1, 0)).astype(bf16)
-    gate = jnp.concatenate(gates, axis=0)
-    w_gu = w_ref[:, : D // 4, :].reshape(D, 2 * FF_E)
-    w_d = w_ref[:, D // 4 :, :].reshape(FF_E, D)
-    x = xs[...]
-    gu = matmul(x, w_gu, (1, 0))
-    g_part, u_part = gu[:, :FF_E], gu[:, FF_E:]
-    sig = 1.0 / (1.0 + jnp.exp(-g_part))
-    act = g_part * sig
-    hid = (act * u_part).astype(bf16)
-    y = matmul(hid, w_d, (1, 0)).astype(bf16).astype(f32)
-    dout = ds[...].astype(f32)
-    dgate = jnp.sum(y * dout, axis=1, keepdims=True)
-    gys[...] = (gate * y).astype(bf16)
-    dy = (gate * dout).astype(bf16)
-    dh = matmul(dy, w_d, (1, 1))
-    da_g = dh * u_part * (sig * (1.0 + g_part * (1.0 - sig)))
-    da = jnp.concatenate([da_g, dh * act], axis=1).astype(bf16)
-    acc_d[...] += matmul(hid, dy, (0, 0))
-    acc_gu[...] += matmul(x, da, (0, 0))
-    dzs[:, :D] = matmul(da, w_gu, (1, 1)).astype(bf16)
-    lane = lax.broadcasted_iota(jnp.int32, (GROUP * CAP, 128), 1)
-    high = dgate.astype(bf16).astype(f32)
-    fields = jnp.where(lane == expert, high, jnp.where(lane == expert + EXPERTS, dgate - high, 0.0))
-    dzs[:, D:] = fields.astype(bf16)
-    slot_lane = lax.broadcasted_iota(jnp.int32, (TOK, CAP), 1).astype(f32)
-    lane_t = lax.broadcasted_iota(jnp.int32, (TOK, 128), 1)
-    for b in range(GROUP):
-        meta = n_ref[b, :, D:].astype(f32)
-        rank = jnp.sum(jnp.where(lane_t == expert, meta, 0.0), axis=1, keepdims=True)
-        spread = jnp.where(slot_lane == rank, 1.0, 0.0).astype(bf16)
-        span = pl.ds(b * CAP, CAP)
-        dn_ref[b] = matmul(spread, dzs[span, :], (1, 0)).astype(bf16)
-        out_ref[b] = matmul(spread, gys[span, :], (1, 0)).astype(bf16)
-
-    @pl.when(step == pl.num_programs(0) - 1)
+        lane = lax.broadcasted_iota(jnp.int32, (16, 128), 1)
+        sub = lax.broadcasted_iota(jnp.int32, (16, 128), 0)
+        wanted = base + 2 * lax.rem(sub, HOSTED) + EXPERTS * (sub // HOSTED)
+        choose = jnp.where((lane == wanted) & (sub < 3 * HOSTED), 1.0, 0.0).astype(bf16)
+        slot = lax.broadcasted_iota(jnp.int32, (CAP, TOK), 0).astype(f32)
+
+        def source(b, carry):
+            fields = matmul(choose, n_ref[b, :, D:], (1, 1))
+            hots = []
+            for j in range(HOSTED):
+                hot = slot == fields[j : j + 1]
+                gate = fields[HOSTED + j : HOSTED + j + 1] + fields[2 * HOSTED + j : 2 * HOSTED + j + 1]
+                span = pl.ds(pl.multiple_of(j * SLOTS + b * CAP, CAP), CAP)
+                gates[span, :] = jnp.broadcast_to(
+                    jnp.sum(jnp.where(hot, gate, 0.0), axis=1, keepdims=True), (CAP, 128)
+                )
+                hots.append(jnp.where(hot, 1.0, 0.0).astype(bf16))
+            hots = jnp.concatenate(hots, axis=0)
+            x = matmul(hots, n_ref[b, :, :D], (1, 0)).astype(bf16)
+            d = matmul(hots, g_ref[b], (1, 0)).astype(bf16)
+            for j in range(HOSTED):
+                span = pl.ds(pl.multiple_of(j * SLOTS + b * CAP, CAP), CAP)
+                xs[span, :] = x[j * CAP : (j + 1) * CAP]
+                ds[span, :] = d[j * CAP : (j + 1) * CAP]
+            return carry
+
+        lax.fori_loop(0, SOURCES, source, 0)
+
+    @pl.when(step < HOSTED)
     def _():
-        dw_ref[:, : D // 4, :] = acc_gu[...].astype(bf16).reshape(4, D // 4, 2 * FF_E)
-        dw_ref[:, D // 4 :, :] = acc_d[...].astype(bf16).reshape(4, FF_E // 4, D)
+        expert = base + 2 * step
+        rows = pl.ds(pl.multiple_of(step * SLOTS, SLOTS), SLOTS)
+        gate = gates[rows, :][:, :1]
+        w_gu = w_ref[0, :, : D // 4, :].reshape(D, 2 * FF_E)
+        w_d = w_ref[0, :, D // 4 :, :].reshape(FF_E, D)
+        gu = matmul(xs[rows, :], w_gu, (1, 0))
+        g_part, u_part = gu[:, :FF_E], gu[:, FF_E:]
+        sig = 1.0 / (1.0 + jnp.exp(-g_part))
+        act = g_part * sig
+        hid = (act * u_part).astype(bf16)
+        y = matmul(hid, w_d, (1, 0)).astype(bf16).astype(f32)
+        dout = ds[rows, :].astype(f32)
+        dgate = jnp.sum(y * dout, axis=1, keepdims=True)
+        dy = (gate * dout).astype(bf16)
+        ds[rows, :] = (gate * y).astype(bf16)
+        dh = matmul(dy, w_d, (1, 1))
+        da_g = dh * u_part * (sig * (1.0 + g_part * (1.0 - sig)))
+        da = jnp.concatenate([da_g, dh * act], axis=1).astype(bf16)
+        dw_ref[0, :, D // 4 :, :] = (
+            matmul(hid, dy, (0, 0)).astype(bf16).reshape(4, FF_E // 4, D)
+        )
+        dw_ref[0, :, : D // 4, :] = (
+            matmul(xs[rows, :], da, (0, 0)).astype(bf16).reshape(4, D // 4, 2 * FF_E)
+        )
+        xs[rows, :] = matmul(da, w_gu, (1, 1)).astype(bf16)
+        lane = lax.broadcasted_iota(jnp.int32, (SLOTS, 128), 1)
+        high = dgate.astype(bf16).astype(f32)
+        fields = jnp.where(lane == expert + EXPERTS, dgate - high, 0.0)
+        zs[rows, :] = jnp.where(lane == expert, high, fields).astype(bf16)
+
+    @pl.when(step >= HOSTED)
+    def _():
+        slot = lax.broadcasted_iota(jnp.int32, (TOK, HOSTED * CAP), 1)
+        lane = lax.broadcasted_iota(jnp.int32, (TOK, 128), 1)
+        for i in range(OUT_BLOCKS):
+            b = (step - HOSTED) * OUT_BLOCKS + i
+            meta = n_ref[b, :, D:].astype(f32)
+            target = jnp.full((TOK, HOSTED * CAP), -1.0, f32)
+            for j in reversed(range(HOSTED)):
+                mine = lane == base + 2 * j
+                rank = jnp.sum(jnp.where(mine, meta, 0.0), axis=1, keepdims=True)
+                rank = jnp.where(rank < 0.0, -1.0, rank + j * CAP)
+                target = jnp.where(slot < (j + 1) * CAP, rank, target)
+            spread = jnp.where(slot.astype(f32) == target, 1.0, 0.0).astype(bf16)
+            spans = [pl.ds(pl.multiple_of(j * SLOTS + b * CAP, CAP), CAP) for j in range(HOSTED)]
+            for ref, out in ((xs, dn_ref.at[i, :, :D]), (zs, dn_ref.at[i, :, D:]), (ds, out_ref.at[i])):
+                rows = jnp.concatenate([ref[span, :] for span in spans], axis=0)
+                out[...] = matmul(spread, rows, (1, 0)).astype(bf16)
 
 
 def experts(n_all, g_all, weights):
-    sources = n_all.shape[0]
     wide = n_all.shape[2]
-    rows = GROUP * CAP
+    slots = HOSTED * SLOTS
 
     def block(width):
-        return pl.BlockSpec((GROUP, TOK, width), lambda i: (i, 0, 0))
+        return pl.BlockSpec(
+            (OUT_BLOCKS, TOK, width), lambda i: (jnp.maximum(i - HOSTED, 0), 0, 0)
+        )
 
     def fixed(shape):
         return pl.BlockSpec(shape, lambda i: (0, 0, 0), pipeline_mode=pl.Buffered(1))
 
+    def one(shape):
+        return pl.BlockSpec((1,) + shape[1:], lambda i: (jnp.minimum(i, HOSTED - 1), 0, 0, 0))
+
     return pl.pallas_call(
         expert_kernel,
-        grid=(sources // GROUP,),
+        grid=(HOSTED + SOURCES // OUT_BLOCKS,),
         out_shape=[
             jax.ShapeDtypeStruct(n_all.shape, bf16),
             jax.ShapeDtypeStruct(g_all.shape, bf16),
             jax.ShapeDtypeStruct(weights.shape, bf16),
         ],
-        in_specs=[block(wide), block(D), fixed(weights.shape)],
-        out_specs=[block(wide), block(D), fixed(weights.shape)],
+        in_specs=[fixed(n_all.shape), fixed(g_all.shape), one(weights.shape)],
+        out_specs=[block(wide), block(D), one(weights.shape)],
         scratch_shapes=[
-            pltpu.VMEM((rows, D), bf16),
-            pltpu.VMEM((rows, D), bf16),
-            pltpu.VMEM((rows, wide), bf16),
-            pltpu.VMEM((rows, D), bf16),
-            pltpu.VMEM((D, 2 * FF_E), f32),
-            pltpu.VMEM((FF_E, D), f32),
+            pltpu.VMEM((slots, D), bf16),
+            pltpu.VMEM((slots, D), bf16),
+            pltpu.VMEM((slots, 128), bf16),
+            pltpu.VMEM((slots, 128), f32),
         ],
         compiler_params=pltpu.CompilerParams(
-            dimension_semantics=("arbitrary",), vmem_limit_bytes=58 * 1024 * 1024
+            dimension_semantics=("arbitrary",), vmem_limit_bytes=62 * 1024 * 1024
         ),
         cost_estimate=pl.CostEstimate(
-            flops=sources * CAP * D * FF_E * 18, bytes_accessed=75_000_000, transcendentals=0
+            flops=slots * D * FF_E * 18, bytes_accessed=45_000_000, transcendentals=0
         ),
         name="experts",
     )(n_all, g_all, weights)
@@ -728,7 +741,7 @@
     n_out, n1_out, q_out, kv_out, lse_out, ho_out, r_out, gate_out, wq, wkv, wo, small_out,
     bias,
 ):
-    z = lax.axis_index("seq")
+    z = lax.axis_index("z")
     unpack_into(wkv, wkv_p)
     unpack_into(wq, wq_p)
 
@@ -864,7 +877,7 @@
     dwq_p, dwkv_p, dwo_p, dn1_out, dr_out,
     bias, square, dkv_t, dq_s, do_s, dkv_s,
 ):
-    z = lax.axis_index("seq")
+    z = lax.axis_index("z")
     own = pl.ds(pl.multiple_of(z * TOK, TOK), TOK)
     gains = gain_rows(small[...])
     lane = lax.broadcasted_iota(jnp.int32, (TOK, 128), 1)
@@ -1009,17 +1022,18 @@
         [router_weight, norm_gains.T, jnp.zeros((8, 128 - EXPERTS - 2), f32)], axis=1
     )
     small = jnp.concatenate([small, jnp.zeros((8, 128), f32)], axis=0)
-    w_q, w_kv, w_o, all_tokens = gather_front(
+    expert_b = lax.all_gather(
+        jnp.concatenate([gateup_weight[0], down_weight[0]], axis=0).astype(bf16),
+        ("y", "z"),
+        axis=0,
+    )
+    w_q, w_kv, w_o, all_tokens, dout_all = gather_front(
         pack_matrix(query_weight).astype(bf16),
         pack_matrix(keyval_weight).astype(bf16),
         jnp.concatenate([pack_matrix(output_weight), small], axis=1).astype(bf16),
         tokens,
-    )
-    expert_b = lax.all_gather(
-        jnp.concatenate([gateup_weight[0], down_weight[0]], axis=0).astype(bf16), "seq", axis=0
-    )
-    dout_all = lax.all_gather(out_grad, "dp", axis=0)
-
+        out_grad,
+    )
     cos, sin = rotary_tables(jnp.arange(seq_len, dtype=jnp.int32), HEAD_DIM // 2)
     cos2, sin2 = jnp.tile(cos, (1, 2)), jnp.tile(sin, (1, 2))
     n_ext, n1, q, kv, lse, ho, residual, gate, query_b, keyval_b, output_b, small_b = front(
@@ -1032,27 +1046,34 @@
         cos2,
         sin2,
     )
-    n_all = gather_plane(n_ext, 2)
+    n_all = gather_rows(n_ext)
     wide = n_all.shape[-1]
     dn_parts, out_parts, d_expert = experts(
-        n_all.reshape(EXPERTS, row_count, wide), dout_all, expert_b
-    )
-    grad_expert = lax.psum_scatter(d_expert, "seq", scatter_dimension=0, tiled=False).astype(f32)
-    sums = sum_plane(dn_parts.reshape(4, 4, 2, row_count, wide), 3, f32)
-    mixed_out = sum_plane(out_parts.reshape(4, 4, 2, row_count, D), 5, f32)
-    layer_out = (residual + mixed_out).astype(bf16)
+        n_all.reshape(SOURCES, row_count, wide),
+        dout_all.reshape(SOURCES, row_count, D),
+        expert_b.reshape((4,) + (4, D // 4 + FF_E // 4, D)),
+    )
+    grad_expert = lax.psum_scatter(
+        d_expert.reshape((16,) + d_expert.shape[2:]),
+        ("y", "z"),
+        scatter_dimension=0,
+        tiled=False,
+    ).astype(f32)
+    sums = sum_rows(dn_parts.reshape(4, 2, row_count, wide))
     d_query, d_keyval, d_last, dn1, dresidual = back(
         lengths, sums, out_grad, n_ext, residual, gate, ho, q, kv, lse, n1, all_tokens,
         query_b, keyval_b, output_b, small_b, cos2, sin2, cos.T, sin.T,
     )
-    g_query, g_keyval, g_last, dn1_sum = sum_back(
+    g_query, g_keyval, g_last, dn1_sum, mixed_out = sum_back(
         (
             d_query.reshape(4, 4, 2, 4, 16, 512),
             d_keyval.reshape(4, 4, 2, 4, 16, 512),
             d_last.reshape(4, 4, 2, 4, 16, 640),
         ),
         dn1,
-    )
+        out_parts.reshape(4, 2, row_count, D),
+    )
+    layer_out = (residual + mixed_out).astype(bf16)
     grad_query, grad_keyval, grad_output = (
         unpack_matrix(g) for g in (g_query, g_keyval, g_last[:, :512])
     )
@@ -1109,13 +1130,18 @@
 
 
 def solution(mesh):
-    rows = P(("dp", "seq"), None)
-    gains = P(None, ("dp", "seq"))
-    shard = P("dp", "seq", None)
+    devices = jax.sharding.Mesh(mesh.devices.reshape(4, 4, 2, 4), ("x", "y", "c", "z"))
+    every = ("x", "y", "c", "z")
+    rows = P(every, None)
+    gains = P(None, every)
+    shard = P(("x", "y", "c"), "z", None)
     return jax.shard_map(
         body,
-        mesh=mesh,
-        in_specs=(rows, rows, P("dp"), rows) + (rows,) * 12 + (gains,) * 3 + (shard,) * 6,
+        mesh=devices,
+        in_specs=(rows, rows, P(("x", "y", "c")), rows)
+        + (rows,) * 12
+        + (gains,) * 3
+        + (shard,) * 6,
         out_specs=(rows, rows) + (rows,) * 12 + (gains,) * 3 + (shard,) * 6,
         check_vma=False,
     )

time: 484 us -> 370 us (0.76)
  Pallas kernels: 444 us -> 326 us
    pallas_call x5 -> x4, Pallas kernels: 341 us -> 211 us  [the longest x1 84.9 us: gather_front(): pl.pallas_call(gather_front_kernel, out_shape=shapes, in_specs=[far] * 5,...]
    pallas_call x1, Pallas kernels: 46.7 us -> 58.9 us  [sum_back(): pl.pallas_call(sum_back_kernel, out_shape=[jax.ShapeDtypeStruct((16, w),...]
  transfers between devices with their start and end apart: 3 -> 2, of which waited for: 0 -> 0; matrix products, arithmetic and copies ran while one was open for 3% -> 5% of each run, Pallas kernels for 79% -> 74%
where the time goes in v2:
time: 370 us
  Pallas kernels  326 us (88%)
  other arithmetic  19.7 us (5%)
  between operations  15.1 us (4%)
  local copies, waits for them, and re-layouts  8.53 us (2%)
    pallas_call x1, Pallas kernels, gather_front(): pl.pallas_call(gather_front_kernel, out_shape=shapes, in_specs=[far] * 5,...  84.9 us
    pallas_call x1, Pallas kernels, sum_back(): pl.pallas_call(sum_back_kernel, out_shape=[jax.ShapeDtypeStruct((16, w),...  58.9 us
    pallas_call x1, Pallas kernels, experts(): pl.pallas_call(expert_kernel, grid=(HOSTED + SOURCES // OUT_BLOCKS,), out...  52.4 us
    pallas_call x1, Pallas kernels, gather_rows(): pl.pallas_call(gather_rows_kernel, out_shape=pltpu.HBM((4, 2) + n.shape,...  44.8 us
    pallas_call x1, Pallas kernels, back(): pl.pallas_call(back_kernel, out_shape=[jax.ShapeDtypeStruct((128, 16, 512...  32.4 us
    pallas_call x1, Pallas kernels, sum_rows(): pl.pallas_call(sum_rows_kernel, out_shape=jax.ShapeDtypeStruct((rows, wid...  28.8 us
    pallas_call x1, Pallas kernels, front(): pl.pallas_call(front_kernel, out_shape=[jax.ShapeDtypeStruct((TOK, D + 12...  23.9 us
    sub x7, other arithmetic, adamw(): return (weight - rate * (update + decay * weight), first_new, second_new)  7.97 us
  transfers between devices with their start and end apart: 2, of which 0 were waited for; matrix products, arithmetic and copies ran while one was open for 5% of the time, Pallas kernels for 74%

profile of v2, /device:TPU:0, one launch (start us, length us, event | category | flops | bytes accessed | tf_op | source)
XLA Modules:
  0.0 369.6 jit_solution(3400762296309074567)
XLA Ops:
  7.3 1.3 convert.43
  8.6 1.1 convert.44
  9.7 0.9 pad_maximum_fusion
  11.4 0.9 fusion.16
  12.4 1.0 copy.87.cos
  13.4 1.0 copy.88.sin
  15.1 0.8 copy.86.routes
  16.6 0.6 pad_maximum_fusion.6
  17.3 84.9 %gather_front.1 = (bf16[4,4,2,4,16,512]{5,4,3,2,1,0:T(8,128)(2,1)}, bf16[4,4,2,4,16,512]{5,4,3,2,1,0:T(8,128)(2,1)}, bf16[4,4,2,4,16,640]{5,4,3,2,1,0:T(8,128)(2...) custom-call(bf16[16,512]{1,0:T(8,128)(2,1)} %get-tuple-element.214.wq, ...), custom_call_target="tpu_custom_call" | custom-call | tf_op jit(solution)/shard_map/gather_front/pallas_call | solution.py:228
  102.1 23.9 %front.1 = (bf16[256,1152]{1,0:T(8,128)(2,1)}, bf16[1024,1024]{1,0:T(8,128)(2,1)}, bf16[256,1024]{1,0:T(8,128)(2,1)}, bf16[1024,1024]{1,0:T(8,128)(2,1)}, f32[25...) custom-call(s32[1]{0:T(128)S(6)} %copy.98.length, ...), custom_call_target="tpu_custom_call" | custom-call | flops 10000000000 | bytes 30000000 | tf_op jit(solution)/shard_map/front/pallas_call | solution.py:829
  126.1 44.8 %gather_rows.1 = bf16[4,2,256,1152]{3,2,1,0:T(8,128)(2,1)} custom-call(bf16[256,1152]{1,0:T(8,128)(2,1)} %get-tuple-element.58.n.n_ext), custom_call_target="tpu_custom_call" | custom-call | tf_op jit(solution)/shard_map/gather_rows/pallas_call | solution.py:249
  171.0 52.4 %experts.1 = (bf16[8,256,1152]{2,1,0:T(8,128)(2,1)}, bf16[8,256,1024]{2,1,0:T(8,128)(2,1)}, bf16[4,4,384,1024]{3,2,1,0:T(8,128)(2,1)}) custom-call(bf16[8,256,1152]{2,1,0:T(8,128)(2,1)} %bitcast.61, bf16[8,256,1024]{2,1,0:T(8,128)(2,1)} %bitcast.70, bf16[4,4,384,1024]{3,2,1,0:T(8,128)(2,1)} %bitcast.69), custom_call_target="tpu_custom_call" | custom-call | flops 28991029248 | bytes 45000000 | tf_op jit(solution)/shard_map/experts/pallas_call | solution.py:673
  224.8 28.8 %sum_rows.1.sums = f32[256,1152]{1,0:T(8,128)} custom-call(bf16[4,2,256,1152]{3,2,1,0:T(8,128)(2,1)} %bitcast.60), custom_call_target="tpu_custom_call" | custom-call | tf_op jit(solution)/shard_map/sum_rows/pallas_call | solution.py:341
  253.6 32.4 %back.1 = (bf16[128,16,512]{2,1,0:T(8,128)(2,1)}, bf16[128,16,512]{2,1,0:T(8,128)(2,1)}, bf16[128,16,640]{2,1,0:T(8,128)(2,1)}, bf16[4,256,1024]{2,1,0:T(8,128)(2,1)}, f32[256,1024]{1,0:T(8,128)}) custom-call(s32[1]{0:T(128)S(6)} %copy.98.length, f32[256,1152]{1,0:T(8,128)} %sum_rows.1.sums, bf16[256,1024]{1,0:T(8,128)(2,1)} %dout.3, ...), custom_call_target="tpu_custom_call" | custom-call | flops 20000000000 | bytes 40000000 | tf_op jit(solution)/shard_map/back/pallas_call | solution.py:971
  286.1 58.9 %sum_back.1 = (f32[16,512]{1,0:T(8,128)}, f32[16,512]{1,0:T(8,128)}, f32[16,640]{1,0:T(8,128)}, f32[256,1024]{1,0:T(8,128)}, f32[256,1024]{1,0:T(8,128)}) custom-call(bf16[4,4,2,4,16,512]{5,4,3,2,1,0:T(8,128)(2,1)} %bitcast.64, bf16[4,4,2,4,16,512]{5,4,3,2,1,0:T(8,128)(2,1)} %bitcast.65, bf16[4,4,2,4,16,640]{5,4,3,2,1,0:T(8,128)(2,1)} %bitcast.63, ...), custom_call_target="tpu_custom_call" | custom-call | tf_op jit(solution)/shard_map/sum_back/pallas_call | solution.py:468
  345.1 0.9 multiply_subtract_fusion.5
  346.0 0.6 copy.95
  346.6 0.6 copy.96
  347.3 0.6 copy.97
  347.9 1.5 fusion.2
  349.5 1.4 multiply_subtract_fusion.6
  350.9 0.7 fusion.29
  351.7 0.7 fusion.30
  352.4 0.7 fusion.31
  353.1 0.7 multiply_subtract_fusion.2
  353.8 0.7 multiply_subtract_fusion.3
  354.5 0.7 multiply_subtract_fusion.4
  355.1 0.9 add_convert_fusion
  356.1 1.3 fusion.5
  357.4 1.4 convert_element_type.49
  359.1 2.2 multiply_subtract_fusion
  361.4 1.4 multiply_subtract_fusion.1
  (87 shorter events, 3.5 us)
Async XLA Ops:
  7.2 3.5 copy-start.13
  7.2 3.5 copy-start.14
  7.2 3.5 copy-start.12
  7.2 3.5 copy-start.25
  7.2 3.6 copy-start.21
  7.2 163.7 %all-gather.2.cloned.1.call-start = ((), (), s32[]{:S(2)}) async-start(), calls=%async_computation.1 | async-start | bytes 13369344 | tf_op jit(solution)/shard_map/all_gather | solution.py:1025
  10.6 346.7 %reduce-scatter.4.cloned.1.call-start = ((), (), s32[]{:S(2)}) async-start(), calls=%async_computation.2 | async-start | bytes 13369344
  12.3 2.8 copy-start.22
  223.4 0.7 copy-start.26
  223.4 0.8 copy-start.27
  223.4 1.0 copy-start.11
  223.4 1.2 copy-start
  286.0 63.4 %copy-start.23 = (f32[8,32]{1,0:T(8,128)S(1)}, f32[8,32]{1,0:T(8,128)}, u32[]{:S(2)}) copy-start(f32[8,32]{1,0:T(8,128)} %param.39) | copy-start | bytes 3076
  286.0 63.4 %copy-start.24 = (f32[8,32]{1,0:T(8,128)S(1)}, f32[8,32]{1,0:T(8,128)}, u32[]{:S(2)}) copy-start(f32[8,32]{1,0:T(8,128)} %param.40) | copy-start | bytes 3076
  286.1 67.1 %copy-start.15 = (f32[8,1024]{1,0:T(8,128)S(1)}, f32[8,1024]{1,0:T(8,128)}, u32[]{:S(2)}) copy-start(f32[8,1024]{1,0:T(8,128)} %param.36) | copy-start | bytes 98308
  286.1 67.1 %copy-start.16 = (f32[8,1024]{1,0:T(8,128)S(1)}, f32[8,1024]{1,0:T(8,128)}, u32[]{:S(2)}) copy-start(f32[8,1024]{1,0:T(8,128)} %param.37) | copy-start | bytes 98308
  286.1 67.7 %copy-start.17 = (f32[8,1024]{1,0:T(8,128)S(1)}, f32[8,1024]{1,0:T(8,128)}, u32[]{:S(2)}) copy-start(f32[8,1024]{1,0:T(8,128)} %param.33) | copy-start | bytes 98308
  286.1 67.7 %copy-start.18 = (f32[8,1024]{1,0:T(8,128)S(1)}, f32[8,1024]{1,0:T(8,128)}, u32[]{:S(2)}) copy-start(f32[8,1024]{1,0:T(8,128)} %param.34) | copy-start | bytes 98308
  345.0 9.4 %copy-start.19 = (f32[8,1024]{1,0:T(8,128)S(1)}, f32[8,1024]{1,0:T(8,128)}, u32[]{:S(2)}) copy-start(f32[8,1024]{1,0:T(8,128)} %param.30) | copy-start | bytes 98308
  345.0 9.4 %copy-start.20 = (f32[8,1024]{1,0:T(8,128)S(1)}, f32[8,1024]{1,0:T(8,128)}, u32[]{:S(2)}) copy-start(f32[8,1024]{1,0:T(8,128)} %param.31) | copy-start | bytes 98308
  345.0 10.1 %copy-start.6 = (f32[256,1024]{1,0:T(8,128)S(1)}, f32[256,1024]{1,0:T(8,128)}, u32[]{:S(2)}) copy-start(f32[256,1024]{1,0:T(8,128)} %get-tuple-element.57.r_ref) | copy-start | bytes 3145732
  345.0 10.1 %copy-start.7 = (f32[256,1024]{1,0:T(8,128)S(1)}, f32[256,1024]{1,0:T(8,128)}, u32[]{:S(2)}) copy-start(f32[256,1024]{1,0:T(8,128)} %get-tuple-element.76) | copy-start | bytes 3145732
  349.4 6.6 %copy-start.2 = (f32[256,1024]{1,0:T(8,128)S(1)}, f32[256,1024]{1,0:T(8,128)}, u32[]{:S(2)}) copy-start(f32[256,1024]{1,0:T(8,128)} %get-tuple-element.78) | copy-start | bytes 3145732
  349.4 6.6 %copy-start.8 = (f32[256,1024]{1,0:T(8,128)S(1)}, f32[256,1024]{1,0:T(8,128)}, u32[]{:S(2)}) copy-start(f32[256,1024]{1,0:T(8,128)} %get-tuple-element.77) | copy-start | bytes 3145732
  356.1 2.8 copy-start.5
  357.4 1.5 copy-start.1
  357.4 1.8 copy-start.4
  359.1 2.2 copy-start.3
  359.1 2.2 copy-start.9
  359.1 2.2 copy-start.10
Sparse Core Ops, SparseCore 0:
  10.8 107.0 all-gather.1
  223.5 112.0 reduce-scatter.3

commit v3 on v2

--- a/solution.py
+++ b/solution.py
@@ -116,37 +116,42 @@
     hand_on(2, 1)
 
 
-def row_steps(wires, at, src, out):
-    half = src.shape[0] // 2
-    own = out.at[at["x"], at["c"]]
-    kept = wires.keep(src, own)
+def row_steps(wires, at, held, out):
+    half = held.shape[2] // 2
     sibling = peer(at, "c", 1)
-    across = []
+    other = shift(at, "c", 1)
+    across, kept = [], []
+
+    def hand_on(by, part):
+        rows = pl.ds(part * half, half)
+        unit, theirs = (
+            (shift(at, "x", by), c, rows) for c in (at["c"], other)
+        )
+        across.append((theirs, wires.send(held.at[unit], held.at[unit], sibling)))
+        kept.append(wires.keep(held.at[unit], out.at[unit]))
 
     def spot(by, part):
-        return out.at[shift(at, "x", by), at["c"], pl.ds(part * half, half)]
-
-    def hand_on(by, part):
-        across.append(wires.send(spot(by, part), spot(by, part), sibling))
-
-    kept.wait()
+        return held.at[shift(at, "x", by), at["c"], pl.ds(part * half, half)]
+
     yield from ring_steps(wires, at, "x", spot, hand_on)
     yield
-    for copy in across:
+    for unit, copy in across:
         copy.wait_recv()
-
-
+        kept.append(wires.keep(held.at[unit], out.at[unit]))
+    for copy in kept:
+        copy.wait()
+
+
+ROW_KEPT = 16
 ROW_COPIES = 6 + 8
 
 
-def token_steps(wires, at, src, out):
-    half = src.shape[0] // 2
-    kept = wires.keep(src, out.at[at["z"]])
+def token_steps(wires, at, held):
+    half = held.shape[1] // 2
 
     def spot(by, part):
-        return out.at[shift(at, "z", by), pl.ds(part * half, half)]
-
-    kept.wait()
+        return held.at[shift(at, "z", by), pl.ds(part * half, half)]
+
     yield from ring_steps(wires, at, "z", spot, lambda by, part: None)
 
 
@@ -201,60 +206,6 @@
 
 
 WEIGHT_COPIES = 3 * (3 + 3 + 6 + 8)
-
-
-GATHER_ORDERS = ("zyx", "zxy", "zyx")
-GATHER_SCHEDULE = "wtdwwdtwdwtd"
-
-
-def gather_front_kernel(wq, wkv, wo, tok, dout, oq, okv, oo, ot, od, *sems):
-    at = place()
-    wires = Wires(*sems)
-    greet(at, "xyzc")
-    in_order(
-        GATHER_SCHEDULE,
-        w=weight_steps(wires, at, list(zip((wq, wkv, wo), (oq, okv, oo), GATHER_ORDERS))),
-        t=token_steps(wires, at, tok, ot),
-        d=row_steps(wires, at, dout, od),
-    )
-    wires.finish()
-
-
-def gather_front(wq, wkv, wo, tok, dout):
-    shapes = [pltpu.HBM((4, 4, 2, 4) + w.shape, w.dtype) for w in (wq, wkv, wo)]
-    shapes.append(pltpu.HBM((4,) + tok.shape, tok.dtype))
-    shapes.append(pltpu.HBM((4, 2) + dout.shape, dout.dtype))
-    far = pl.BlockSpec(memory_space=pltpu.HBM)
-    return pl.pallas_call(
-        gather_front_kernel,
-        out_shape=shapes,
-        in_specs=[far] * 5,
-        out_specs=[far] * 5,
-        scratch_shapes=wire_sems(WEIGHT_COPIES + TOKEN_COPIES + ROW_COPIES, 5),
-        compiler_params=pltpu.CompilerParams(collective_id=1, has_side_effects=True),
-        name="gather_front",
-    )(*hbm(wq, wkv, wo, tok, dout))
-
-
-def gather_rows_kernel(n, o, *sems):
-    at = place()
-    wires = Wires(*sems)
-    greet(at, "xc")
-    in_order("", d=row_steps(wires, at, n, o))
-    wires.finish()
-
-
-def gather_rows(n):
-    far = pl.BlockSpec(memory_space=pltpu.HBM)
-    return pl.pallas_call(
-        gather_rows_kernel,
-        out_shape=pltpu.HBM((4, 2) + n.shape, n.dtype),
-        in_specs=[far],
-        out_specs=far,
-        scratch_shapes=wire_sems(ROW_COPIES, 1),
-        compiler_params=pltpu.CompilerParams(collective_id=2, has_side_effects=True),
-        name="gather_rows",
-    )(*hbm(n))
 
 
 def add_rows(out, parts, rows):
@@ -736,14 +687,10 @@
     bias[...] = jnp.where((keys <= rows) & (keys < length), 0.0, masked_score)
 
 
-def front_kernel(
-    length, wq_p, wkv_p, wo_p, tok, routes, cos, sin,
-    n_out, n1_out, q_out, kv_out, lse_out, ho_out, r_out, gate_out, wq, wkv, wo, small_out,
-    bias,
-):
-    z = lax.axis_index("z")
+def front_steps(z, length, wq_p, wkv_p, wo_p, tok, routes, cos, sin, outs, n_held, bias):
+    n_out, n1_out, q_out, kv_out, lse_out, ho_out, r_out, gate_out, wq, wkv, wo, small_out = outs
+    width = KV_HEADS * HEAD_DIM
     unpack_into(wkv, wkv_p)
-    unpack_into(wq, wq_p)
 
     def small_chunk(i, carry):
         x = wo_p[pl.ds(i * 16, 16), :, 512:].astype(f32)
@@ -752,36 +699,34 @@
         return carry
 
     lax.fori_loop(0, 8, small_chunk, 0)
-    unpack_into(wo, wo_p)
     gains = gain_rows(small_out[...])
-    fill_bias(bias, length[0], z * TOK)
-    width = KV_HEADS * HEAD_DIM
-
-    def block(b, carry):
+    yield
+    for b in range(4):
         x = tok[b].astype(f32)
         n1 = (x * rms_scale(x) * gains[0:1]).astype(bf16)
-        rows = pl.ds(pl.multiple_of(b * TOK, TOK), TOK)
+        rows = pl.ds(b * TOK, TOK)
         n1_out[rows, :] = n1
         kv = matmul(n1, wkv[...], (1, 0))
         kv_out[rows, :width] = turned_rows(
             kv[:, :width], cos[rows, :], sin[rows, :], False
         ).astype(bf16)
         kv_out[rows, width:] = kv[:, width:].astype(bf16)
-        return carry
-
-    lax.fori_loop(0, 4, block, 0)
+        yield
+    unpack_into(wq, wq_p)
     own = pl.ds(pl.multiple_of(z * TOK, TOK), TOK)
     q = matmul(n1_out[own, :], wq[...], (1, 0))
     q = turned_rows(q, cos[own, :], sin[own, :], False).astype(bf16)
     q_out[...] = q * jnp.asarray(HEAD_DIM ** (-0.5), bf16)
     lse_out[...] = jnp.zeros_like(lse_out)
+    fill_bias(bias, length[0], z * TOK)
     lane = lax.broadcasted_iota(jnp.int32, (TOK, 128), 1)
-
-    def heads(j, carry):
-        keys = kv_out[:, pl.ds(pl.multiple_of(j * 128, 128), 128)]
-        values = kv_out[:, pl.ds(pl.multiple_of(width + j * 128, 128), 128)]
+    yield
+
+    def heads(j):
+        keys = kv_out[:, pl.ds(j * 128, 128)]
+        values = kv_out[:, pl.ds(width + j * 128, 128)]
         for g in (0, 1):
-            span = pl.ds(pl.multiple_of(j * 256 + g * 128, 128), 128)
+            span = pl.ds(j * 256 + g * 128, 128)
             qs = q_out[:, span]
             key = keys[:, g * HEAD_DIM : (g + 1) * HEAD_DIM]
             value = values[:, g * HEAD_DIM : (g + 1) * HEAD_DIM]
@@ -796,13 +741,16 @@
                 head = j * 4 + g * 2 + h
                 lse_out[...] = jnp.where(lane == head, top + jnp.log(total), lse_out[...])
             ho_out[:, span] = jnp.concatenate(mixed, axis=1).astype(bf16)
-        return carry
-
-    lax.fori_loop(0, 4, heads, 0)
+
+    for j in range(4):
+        heads(j)
+        yield
+    unpack_into(wo, wo_p)
     r = tok[z].astype(f32) + matmul(ho_out[...], wo[...], (1, 0))
     r_out[...] = r
     n2 = (r * rms_scale(r) * gains[1:2]).astype(bf16)
     n_out[:, :D] = n2
+    n_held[:, :D] = n2
     logits = matmul(n2, small_out[...], (1, 0))
     hits = lane == routes[:, 0:1]
     for k in range(1, routes.shape[1]):
@@ -818,14 +766,68 @@
     high = gate.astype(bf16).astype(f32)
     meta = jnp.where(hits, ranks, jnp.where(lane < EXPERTS, -1.0, 0.0))
     meta = meta + pltpu.roll(high, EXPERTS, 1) + pltpu.roll(gate - high, 2 * EXPERTS, 1)
-    n_out[:, D:] = meta.astype(bf16)
-
-
-def front(length, w_q, w_kv, w_o, tok, routes, cos, sin):
+    meta = meta.astype(bf16)
+    n_out[:, D:] = meta
+    n_held[:, D:] = meta
+
+
+GATHER_ORDERS = ("zyx", "yzx", "zyx")
+FRONT_SCHEDULE = "wtwwtwdtwwt" + "fd" * 6 + "f" * 12
+
+
+def front_kernel(
+    length, w_kv, w_q, w_o, tok, dout, routes, cos, sin,
+    n_out, n1_out, q_out, kv_out, lse_out, ho_out, r_out, gate_out, wq, wkv, wo, small_out,
+    tok_out, dout_out, n_all,
+    wkv_p, wq_p, wo_p, tok_held, dout_held, n_held, bias, *sems,
+):
+    at = place()
+    wires = Wires(*sems)
+    own_tok = wires.keep(tok, tok_held.at[at["z"]])
+    own_dout = wires.keep(dout, dout_held.at[at["x"], at["c"]])
+    weights = weight_steps(
+        wires, at, list(zip((w_kv, w_q, w_o), (wkv_p, wq_p, wo_p), GATHER_ORDERS))
+    )
+    tokens = token_steps(wires, at, tok_held)
+    flat = [p.reshape(128, *p.shape[-2:]) for p in (wq_p, wkv_p, wo_p)]
+    outs = (
+        n_out, n1_out, q_out, kv_out, lse_out, ho_out, r_out, gate_out, wq, wkv, wo, small_out
+    )
+
+    def forward():
+        for _ in weights:
+            pass
+        for _ in tokens:
+            pass
+        kept = wires.keep(tok_held, tok_out)
+        yield from front_steps(
+            at["z"], length, *flat, tok_held, routes, cos, sin, outs,
+            n_held.at[at["x"], at["c"]], bias,
+        )
+        kept.wait()
+
+    greet(at, "xyzc")
+    own_tok.wait()
+    own_dout.wait()
+    in_order(
+        FRONT_SCHEDULE,
+        w=weights,
+        t=tokens,
+        d=row_steps(wires, at, dout_held, dout_out),
+        f=forward(),
+    )
+    in_order("", n=row_steps(wires, at, n_held, n_all))
+    wires.finish()
+
+
+def front(length, w_q, w_kv, w_o, tok, dout, routes, cos, sin):
     vmem = pl.BlockSpec(memory_space=pltpu.VMEM)
+    far = pl.BlockSpec(memory_space=pltpu.HBM)
     square = jax.ShapeDtypeStruct((D, D), bf16)
     rows = jax.ShapeDtypeStruct((TOK, D), bf16)
     lanes = jax.ShapeDtypeStruct((TOK, 128), f32)
+    lead = (4, 4, 2, 4)
+    copies = WEIGHT_COPIES + TOKEN_COPIES + 2 * ROW_COPIES
     return pl.pallas_call(
         front_kernel,
         out_shape=[
@@ -841,16 +843,30 @@
             square,
             square,
             jax.ShapeDtypeStruct((D, 128), bf16),
+            pltpu.HBM((4, TOK, D), bf16),
+            pltpu.HBM((4, 2, TOK, D), bf16),
+            pltpu.HBM((4, 2, TOK, D + 128), bf16),
         ],
-        in_specs=[pl.BlockSpec(memory_space=pltpu.SMEM)] + [vmem] * 7,
-        out_specs=[vmem] * 12,
-        scratch_shapes=[pltpu.VMEM((TOK, 4 * TOK), f32)],
-        compiler_params=pltpu.CompilerParams(vmem_limit_bytes=56 * 1024 * 1024),
+        in_specs=[pl.BlockSpec(memory_space=pltpu.SMEM)] + [far] * 5 + [vmem] * 3,
+        out_specs=[vmem] * 12 + [far] * 3,
+        scratch_shapes=[
+            pltpu.VMEM(lead + w_kv.shape, bf16),
+            pltpu.VMEM(lead + w_q.shape, bf16),
+            pltpu.VMEM(lead + w_o.shape, bf16),
+            pltpu.VMEM((4, TOK, D), bf16),
+            pltpu.VMEM((4, 2, TOK, D), bf16),
+            pltpu.VMEM((4, 2, TOK, D + 128), bf16),
+            pltpu.VMEM((TOK, 4 * TOK), f32),
+        ]
+        + wire_sems(copies, 2 + 3 + 1 + 2 * ROW_KEPT),
+        compiler_params=pltpu.CompilerParams(
+            collective_id=1, has_side_effects=True, vmem_limit_bytes=60 * 1024 * 1024
+        ),
         cost_estimate=pl.CostEstimate(
             flops=10**10, bytes_accessed=30_000_000, transcendentals=5_000_000
         ),
         name="front",
-    )(length, w_q, w_kv, w_o, tok, routes, cos, sin)
+    )(length, *hbm(w_kv, w_q, w_o, tok, dout), routes, cos, sin)
 
 
 def rms_back(values, scale, gain, dnormed):
@@ -1027,26 +1043,22 @@
         ("y", "z"),
         axis=0,
     )
-    w_q, w_kv, w_o, all_tokens, dout_all = gather_front(
+    cos, sin = rotary_tables(jnp.arange(seq_len, dtype=jnp.int32), HEAD_DIM // 2)
+    cos2, sin2 = jnp.tile(cos, (1, 2)), jnp.tile(sin, (1, 2))
+    (
+        n_ext, n1, q, kv, lse, ho, residual, gate, query_b, keyval_b, output_b, small_b,
+        all_tokens, dout_all, n_all,
+    ) = front(
+        lengths,
         pack_matrix(query_weight).astype(bf16),
         pack_matrix(keyval_weight).astype(bf16),
         jnp.concatenate([pack_matrix(output_weight), small], axis=1).astype(bf16),
         tokens,
         out_grad,
-    )
-    cos, sin = rotary_tables(jnp.arange(seq_len, dtype=jnp.int32), HEAD_DIM // 2)
-    cos2, sin2 = jnp.tile(cos, (1, 2)), jnp.tile(sin, (1, 2))
-    n_ext, n1, q, kv, lse, ho, residual, gate, query_b, keyval_b, output_b, small_b = front(
-        lengths,
-        w_q.reshape(128, 16, 512),
-        w_kv.reshape(128, 16, 512),
-        w_o.reshape(128, 16, 640),
-        all_tokens,
         routes,
         cos2,
         sin2,
     )
-    n_all = gather_rows(n_ext)
     wide = n_all.shape[-1]
     dn_parts, out_parts, d_expert = experts(
         n_all.reshape(SOURCES, row_count, wide),

time: 370 us -> 345 us (0.932); the launches traced: 370 us -> 340 us
  Pallas kernels: 326 us -> 296 us
    pallas_call x2 -> x0, Pallas kernels: 130 us -> none  [the longest x1 84.9 us: gather_front(): pl.pallas_call(gather_front_kernel, out_shape=shapes, in_specs=[far] * 5,...]
    pallas_call x1, Pallas kernels: 23.9 us -> 124 us  [front(): pl.pallas_call(front_kernel, out_shape=[jax.ShapeDtypeStruct((TOK, D + 12...]
  transfers between devices with their start and end apart: 2 -> 2, of which waited for: 0 -> 0; matrix products, arithmetic and copies ran while one was open for 5% -> 6% of each run, Pallas kernels for 74% -> 72%
where the time goes in v3:
time: 345 us; the launch traced here: 340 us
  Pallas kernels  296 us (86%)
  other arithmetic  19.7 us (6%)
  between operations  15.6 us (5%)
  local copies, waits for them, and re-layouts  8.54 us (2%)
    pallas_call x1, Pallas kernels, front(): pl.pallas_call(front_kernel, out_shape=[jax.ShapeDtypeStruct((TOK, D + 12...  124 us
    pallas_call x1, Pallas kernels, sum_back(): pl.pallas_call(sum_back_kernel, out_shape=[jax.ShapeDtypeStruct((16, w),...  57.3 us
    pallas_call x1, Pallas kernels, experts(): pl.pallas_call(expert_kernel, grid=(HOSTED + SOURCES // OUT_BLOCKS,), out...  52.3 us
    pallas_call x1, Pallas kernels, back(): pl.pallas_call(back_kernel, out_shape=[jax.ShapeDtypeStruct((128, 16, 512...  32.4 us
    pallas_call x1, Pallas kernels, sum_rows(): pl.pallas_call(sum_rows_kernel, out_shape=jax.ShapeDtypeStruct((rows, wid...  29.5 us
    sub x7, other arithmetic, adamw(): return (weight - rate * (update + decay * weight), first_new, second_new)  7.95 us
  transfers between devices with their start and end apart: 2, of which 0 were waited for; matrix products, arithmetic and copies ran while one was open for 6% of the time, Pallas kernels for 72%

profile of v3, /device:TPU:0, one launch (start us, length us, event | category | flops | bytes accessed | tf_op | source)
XLA Modules:
  0.0 339.7 jit_solution(17822550997670136643)
XLA Ops:
  7.2 1.3 convert.43
  8.5 1.1 convert.44
  9.6 0.9 pad_maximum_fusion
  11.2 0.9 fusion.16
  12.2 1.0 copy.87.cos
  13.2 1.0 copy.88.sin
  15.1 0.8 copy.86.routes
  16.0 0.6 fusion.15.w_o
  16.6 0.6 pad_maximum_fusion.6
  17.3 124.3 %front.1 = (bf16[256,1152]{1,0:T(8,128)(2,1)}, bf16[1024,1024]{1,0:T(8,128)(2,1)}, bf16[256,1024]{1,0:T(8,128)(2,1)}, bf16[1024,1024]{1,0:T(8,128)(2,1)}, f32[25...) custom-call(s32[1]{0:T(128)S(6)} %copy.98.length, ...), custom_call_target="tpu_custom_call" | custom-call | flops 10000000000 | bytes 30000000 | tf_op jit(solution)/shard_map/front/pallas_call | solution.py:831
  141.6 52.3 %experts.1 = (bf16[8,256,1152]{2,1,0:T(8,128)(2,1)}, bf16[8,256,1024]{2,1,0:T(8,128)(2,1)}, bf16[4,4,384,1024]{3,2,1,0:T(8,128)(2,1)}) custom-call(bf16[8,256,1152]{2,1,0:T(8,128)(2,1)} %bitcast.66, bf16[8,256,1024]{2,1,0:T(8,128)(2,1)} %bitcast.67, bf16[4,4,384,1024]{3,2,1,0:T(8,128)(2,1)} %bitcast.65), custom_call_target="tpu_custom_call" | custom-call | flops 28991029248 | bytes 45000000 | tf_op jit(solution)/shard_map/experts/pallas_call | solution.py:624
  194.1 0.6 copy-done.26
  195.3 29.5 %sum_rows.1.sums = f32[256,1152]{1,0:T(8,128)} custom-call(bf16[4,2,256,1152]{3,2,1,0:T(8,128)(2,1)} %bitcast.57), custom_call_target="tpu_custom_call" | custom-call | tf_op jit(solution)/shard_map/sum_rows/pallas_call | solution.py:292
  224.9 32.4 %back.1 = (bf16[128,16,512]{2,1,0:T(8,128)(2,1)}, bf16[128,16,512]{2,1,0:T(8,128)(2,1)}, bf16[128,16,640]{2,1,0:T(8,128)(2,1)}, bf16[4,256,1024]{2,1,0:T(8,128)(2,1)}, f32[256,1024]{1,0:T(8,128)}) custom-call(s32[1]{0:T(128)S(6)} %copy.98.length, f32[256,1152]{1,0:T(8,128)} %sum_rows.1.sums, bf16[256,1024]{1,0:T(8,128)(2,1)} %dout.3, ...), custom_call_target="tpu_custom_call" | custom-call | flops 20000000000 | bytes 40000000 | tf_op jit(solution)/shard_map/back/pallas_call | solution.py:987
  257.3 57.3 %sum_back.1 = (f32[16,512]{1,0:T(8,128)}, f32[16,512]{1,0:T(8,128)}, f32[16,640]{1,0:T(8,128)}, f32[256,1024]{1,0:T(8,128)}, f32[256,1024]{1,0:T(8,128)}) custom-call(bf16[4,4,2,4,16,512]{5,4,3,2,1,0:T(8,128)(2,1)} %bitcast.60, bf16[4,4,2,4,16,512]{5,4,3,2,1,0:T(8,128)(2,1)} %bitcast.61, bf16[4,4,2,4,16,640]{5,4,3,2,1,0:T(8,128)(2,1)} %bitcast.59, ...), custom_call_target="tpu_custom_call" | custom-call | tf_op jit(solution)/shard_map/sum_back/pallas_call | solution.py:419
  314.7 0.9 multiply_subtract_fusion.5
  315.6 0.6 copy.95
  316.2 0.6 copy.96
  316.9 0.6 copy.97
  317.5 1.5 fusion.2
  319.1 1.4 multiply_subtract_fusion.6
  320.5 0.7 fusion.29
  321.3 0.7 fusion.30
  322.0 0.7 fusion.31
  322.7 0.7 multiply_subtract_fusion.2
  323.4 0.7 multiply_subtract_fusion.3
  324.1 0.7 multiply_subtract_fusion.4
  324.7 0.9 add_convert_fusion
  325.7 1.3 fusion.5
  327.0 1.4 convert_element_type.49
  328.7 2.2 multiply_subtract_fusion
  331.0 1.4 multiply_subtract_fusion.1
  (85 shorter events, 2.3 us)
Async XLA Ops:
  7.2 134.4 %all-gather.2.cloned.1.call-start = ((), (), s32[]{:S(2)}) async-start(), calls=%async_computation.1 | async-start | bytes 13369344 | tf_op jit(solution)/shard_map/all_gather | solution.py:1041
  10.6 316.4 %reduce-scatter.4.cloned.1.call-start = ((), (), s32[]{:S(2)}) async-start(), calls=%async_computation.2 | async-start | bytes 13369344
  12.1 2.1 copy-start.14
  12.1 2.1 copy-start.13
  12.1 2.2 copy-start.12
  12.1 2.2 copy-start.25
  12.1 2.3 copy-start.21
  12.1 2.9 copy-start.22
  193.9 0.7 copy-start.26
  193.9 0.8 copy-start.27
  193.9 1.0 copy-start.11
  193.9 1.2 copy-start
  257.3 61.8 %copy-start.23 = (f32[8,32]{1,0:T(8,128)S(1)}, f32[8,32]{1,0:T(8,128)}, u32[]{:S(2)}) copy-start(f32[8,32]{1,0:T(8,128)} %param.39) | copy-start | bytes 3076
  257.3 61.8 %copy-start.24 = (f32[8,32]{1,0:T(8,128)S(1)}, f32[8,32]{1,0:T(8,128)}, u32[]{:S(2)}) copy-start(f32[8,32]{1,0:T(8,128)} %param.40) | copy-start | bytes 3076
  257.3 65.5 %copy-start.15 = (f32[8,1024]{1,0:T(8,128)S(1)}, f32[8,1024]{1,0:T(8,128)}, u32[]{:S(2)}) copy-start(f32[8,1024]{1,0:T(8,128)} %param.36) | copy-start | bytes 98308
  257.3 65.4 %copy-start.16 = (f32[8,1024]{1,0:T(8,128)S(1)}, f32[8,1024]{1,0:T(8,128)}, u32[]{:S(2)}) copy-start(f32[8,1024]{1,0:T(8,128)} %param.37) | copy-start | bytes 98308
  257.3 66.1 %copy-start.17 = (f32[8,1024]{1,0:T(8,128)S(1)}, f32[8,1024]{1,0:T(8,128)}, u32[]{:S(2)}) copy-start(f32[8,1024]{1,0:T(8,128)} %param.33) | copy-start | bytes 98308
  257.3 66.1 %copy-start.18 = (f32[8,1024]{1,0:T(8,128)S(1)}, f32[8,1024]{1,0:T(8,128)}, u32[]{:S(2)}) copy-start(f32[8,1024]{1,0:T(8,128)} %param.34) | copy-start | bytes 98308
  314.6 9.4 %copy-start.19 = (f32[8,1024]{1,0:T(8,128)S(1)}, f32[8,1024]{1,0:T(8,128)}, u32[]{:S(2)}) copy-start(f32[8,1024]{1,0:T(8,128)} %param.30) | copy-start | bytes 98308
  314.7 9.4 %copy-start.20 = (f32[8,1024]{1,0:T(8,128)S(1)}, f32[8,1024]{1,0:T(8,128)}, u32[]{:S(2)}) copy-start(f32[8,1024]{1,0:T(8,128)} %param.31) | copy-start | bytes 98308
  314.7 10.1 %copy-start.6 = (f32[256,1024]{1,0:T(8,128)S(1)}, f32[256,1024]{1,0:T(8,128)}, u32[]{:S(2)}) copy-start(f32[256,1024]{1,0:T(8,128)} %get-tuple-element.51.r_ref) | copy-start | bytes 3145732
  314.7 10.0 %copy-start.7 = (f32[256,1024]{1,0:T(8,128)S(1)}, f32[256,1024]{1,0:T(8,128)}, u32[]{:S(2)}) copy-start(f32[256,1024]{1,0:T(8,128)} %get-tuple-element.72) | copy-start | bytes 3145732
  319.0 6.6 %copy-start.2 = (f32[256,1024]{1,0:T(8,128)S(1)}, f32[256,1024]{1,0:T(8,128)}, u32[]{:S(2)}) copy-start(f32[256,1024]{1,0:T(8,128)} %get-tuple-element.74) | copy-start | bytes 3145732
  319.1 6.6 %copy-start.8 = (f32[256,1024]{1,0:T(8,128)S(1)}, f32[256,1024]{1,0:T(8,128)}, u32[]{:S(2)}) copy-start(f32[256,1024]{1,0:T(8,128)} %get-tuple-element.73) | copy-start | bytes 3145732
  325.7 2.8 copy-start.5
  327.0 1.5 copy-start.1
  327.0 1.8 copy-start.4
  328.7 2.2 copy-start.3
  328.7 2.2 copy-start.9
  328.7 2.2 copy-start.10
Sparse Core Ops, SparseCore 0:
  10.8 104.5 all-gather.1
  194.1 111.4 reduce-scatter.3
